TPU v7x, 512 devices: a whole 4x4x16 slice. The times are simulated.
512 devices in a mesh: loop: 32 (over z_hi, x, y), grp: 16 (over z_lo, core).
Axes of the slice: x: 4, y: 4, z: 16 (z_hi: 2, z_lo: 8; z = z_hi * 8 + z_lo), core: 2. Of those that a mesh axis runs over, the one named last changes fastest.
Arguments:
- views: bfloat16 [8192, 1024], P(('loop', 'grp')), may hold values from -2 to 2
- partner: int32 [8192], P(('loop', 'grp')), may hold values from 0 to 8191, as said below
Outputs:
- view_loss: float32 [8192], P(('loop', 'grp'))
- derivative_samples: bfloat16 [8192, 1024], P(('loop', 'grp'))
Inputs may be any that keep to these rules, and one draw needn't show every extreme that they name: partner pairs the views: partner[partner[i]] == i and partner[i] != i.
All inputs are finite; a program needn't handle non-finite values.
Results may differ from a plain program's by a relative error of at most 0.0085.
Values may be sent and summed in bfloat16 or wider, within the bound.
No kernel may reach another device: no remote copies, remote signals or barrier semaphores. Data moves between devices by JAX's collectives and lax.ppermute only.
A program may use at most 64 MiB of HBM per device.

v0:
```python
import jax
import jax.numpy as jnp
from jax import lax
from jax.sharding import PartitionSpec as P

inverse_softness = 10.0
very_low = -1e30


def local(views, partner):
    shard_rows = views.shape[0]
    group_size = lax.axis_size("grp")
    group_pos = lax.axis_index("grp")
    loop_pos = lax.axis_index("loop")
    row_embeddings, rows_partner = (
        lax.all_gather(views, "grp", axis=0, tiled=True),
        lax.all_gather(partner, "grp", axis=0, tiled=True),
    )
    span = group_size * shard_rows
    row_ids = loop_pos * span + jnp.arange(span, dtype=jnp.int32)
    column_embeddings = lax.all_gather(views, "loop", axis=0, tiled=True)
    index = jnp.arange(column_embeddings.shape[0], dtype=jnp.int32)
    column_ids = index // shard_rows * span + group_pos * shard_rows + index % shard_rows
    cosine_logits = inverse_softness * jnp.dot(
        row_embeddings, column_embeddings.T, preferred_element_type=jnp.float32
    )
    self_mask = row_ids[:, None] == column_ids[None, :]
    positive = column_ids[None, :] == rows_partner[:, None]
    masked = jnp.where(self_mask, very_low, cosine_logits)
    maxima = jnp.max(masked, axis=1)
    totals = jnp.sum(jnp.where(self_mask, 0.0, jnp.exp(masked - maxima[:, None])), axis=1)
    picked = jnp.sum(jnp.where(positive, cosine_logits, 0.0), axis=1)
    top = lax.pmax(maxima, "grp")
    totals, picked = lax.psum((totals * jnp.exp(maxima - top), picked), "grp")
    maxima = top
    lse = maxima + jnp.log(totals)
    objective_entries = lse - picked
    local_penalty = lax.dynamic_slice_in_dim(
        objective_entries, group_pos * shard_rows, shard_rows, 0
    )
    probs = jnp.where(self_mask, 0.0, jnp.exp(masked - lse[:, None]))
    weight_matrix = (probs - positive.astype(jnp.float32)).astype(jnp.bfloat16)
    left_multiplier = inverse_softness * jnp.dot(
        weight_matrix, column_embeddings, preferred_element_type=jnp.float32
    )
    row_part = lax.psum_scatter(left_multiplier, "grp", scatter_dimension=0, tiled=True)
    right_multiplier = inverse_softness * lax.dot_general(
        weight_matrix, row_embeddings, (((0,), (0,)), ((), ())), preferred_element_type=jnp.float32
    )
    right_slice = lax.psum_scatter(right_multiplier, "loop", scatter_dimension=0, tiled=True)
    derivative_samples = (row_part + right_slice).astype(jnp.bfloat16)
    return (local_penalty, derivative_samples)


def solution(mesh):
    in_specs = (P(("loop", "grp"), None), P(("loop", "grp")))
    out_specs = (P(("loop", "grp")), P(("loop", "grp"), None))
    return jax.shard_map(local, mesh=mesh, in_specs=in_specs, out_specs=out_specs, check_vma=False)
```

profile of v0, /device:TPU:30, one launch (start us, length us, event | category | flops | bytes accessed | tf_op | source)
XLA Modules:
  0.0 635.7 jit_solution(18098727880895488977)
XLA Ops:
  7.2 0.0 all-gather.2.cloned.1.call-start
  7.2 0.7 all-gather.2.cloned.1.call-update
  7.9 0.0 reduce-scatter.3.cloned.1.call-start
  8.0 1.3 dynamic-slice
  9.9 0.9 dynamic-update-slice
  10.7 19.0 %all-reduce = s32[256]{0:T(256)S(1)} all-reduce(s32[256]{0:T(256)S(1)} %dynamic-update-slice), channel_id=1, replica_groups=mesh['loop'=32,'grp'=16] {'grp'}, use_global_device_ids=true, to_apply=%add | all-reduce | flops 256 | bytes 2048
  29.7 28.2 %all_gather.9 = bf16[256,1024]{1,0:T(8,128)(2,1)S(1)} all-gather(bf16[16,1024]{1,0:T(8,128)(2,1)} %param.2), channel_id=1, replica_groups=mesh['loop'=32,'grp'=16] {'grp'}, dimensions={0}, use_global_device_ids=true | all-gather | bytes 557056 | tf_op jit(solution)/shard_map/all_gather | solution.py:16
  58.0 68.2 %all-gather.2.cloned.1.call-done = bf16[512,1024]{1,0:T(8,128)(2,1)} async-done(((bf16[16,1024]{1,0:T(8,128)(2,1)}), bf16[512,1024]{1,0:T(8,128)(2,1)}) %all-gather.2.cloned.1.call-update) | async-done | bytes 1048592 | tf_op jit(solution)/shard_map/all_gather | solution.py:21
  126.1 0.0 copy-start
  126.1 1.9 fusion.4
  128.0 45.2 %pmax.7 = f32[256]{0:T(256)S(1)} all-reduce(f32[256]{0:T(256)S(1)} %get-tuple-element.8), channel_id=1, replica_groups=mesh['loop'=32,'grp'=16] {'grp'}, use_global_device_ids=true, to_apply=%region_1.2 | all-reduce | flops 256 | bytes 2048 | tf_op jit(solution)/shard_map/pmax | solution.py:33
  173.2 0.3 fusion
  173.6 45.1 %all-reduce.1 = (f32[256]{0:T(256)S(1)}, f32[256]{0:T(256)S(1)}) all-reduce(f32[256]{0:T(256)S(1)} %exponential_multiply_fusion, f32[256]{0:T(256)S(1)} %get-tuple-element.2), channel_id=1, replica_groups=mesh['loop'=32,'grp'=16] {'grp'}, use_global_device_ids=true, to_apply=%region_3.4 | all-reduce | flops 512 | bytes 4096 | tf_op jit(solution)/shard_map/psum | solution.py:34
  218.7 0.0 copy-done
  218.7 1.6 convolution_multiply_fusion.1
  220.3 0.0 reduce-scatter.3.cloned.1.call-update
  220.3 0.0 reduce-scatter.5.cloned.1.call-start
  220.3 2.0 convolution_multiply_fusion
  222.4 0.0 reduce-scatter.5.cloned.1.call-update
  222.4 0.6 dynamic_slice.3
  223.0 96.2 %reduce-scatter.3.cloned.1.call-done = f32[16,1024]{1,0:T(8,128)} async-done(((f32[256,1024]{1,0:T(8,128)}), f32[16,1024]{1,0:T(8,128)}) %reduce-scatter.3.cloned.1.call-update) | async-done | bytes 65552 | tf_op jit(solution)/shard_map/reduce_scatter | solution.py:46
  319.2 308.4 %reduce-scatter.5.cloned.1.call-done = f32[16,1024]{1,0:T(8,128)} async-done(((f32[512,1024]{1,0:T(8,128)}), f32[16,1024]{1,0:T(8,128)}) %reduce-scatter.5.cloned.1.call-update) | async-done | bytes 65552 | tf_op jit(solution)/shard_map/reduce_scatter | solution.py:50
  627.6 1.5 add_convert_fusion
  (5 shorter events, 0.0 us)
Async XLA Ops:
  7.2 119.0 %all-gather.2.cloned.1.call-start = ((), (), s32[]{:S(2)}) async-start(), calls=%async_computation.2 | async-start | bytes 1081344 | tf_op jit(solution)/shard_map/all_gather | solution.py:21
  7.9 311.3 %reduce-scatter.3.cloned.1.call-start = ((), (), s32[]{:S(2)}) async-start(), calls=%async_computation.3 | async-start | bytes 1114112 | tf_op jit(solution)/shard_map/reduce_scatter | solution.py:46
  126.1 92.6 %copy-start = (bf16[512,1024]{1,0:T(8,128)(2,1)S(1)}, bf16[512,1024]{1,0:T(8,128)(2,1)}, u32[]{:S(2)}) copy-start(bf16[512,1024]{1,0:T(8,128)(2,1)} %all-gather.2.cloned.1.call-done) | copy-start | bytes 3145732
  220.3 407.4 %reduce-scatter.5.cloned.1.call-start = ((), (), s32[]{:S(2)}) async-start(), calls=%async_computation.4 | async-start | bytes 2162688 | tf_op jit(solution)/shard_map/reduce_scatter | solution.py:50
Sparse Core Ops, SparseCore 0:
  12.3 113.7 all-gather.1
  220.4 98.7 reduce-scatter.2
  322.2 305.3 reduce-scatter.4
where the time goes:
time: 636 us
  waiting for transfers between devices  474 us (75%)
  blocking collectives  138 us (22%)
  between operations  14.4 us (2%)
    reduce_scatter x1, waiting for transfers between devices, local(): lax.psum_scatter(right_multiplier, 'loop', scatter_dimension=0, tiled=True)  308 us
    reduce_scatter x1, waiting for transfers between devices, local(): lax.psum_scatter(left_multiplier, 'grp', scatter_dimension=0, tiled=True)  96.2 us
    all_gather x1, waiting for transfers between devices, local(): column_embeddings = lax.all_gather(views, 'loop', axis=0, tiled=True)  68.2 us
    pmax x1, blocking collectives, local(): top = lax.pmax(maxima, 'grp')  45.2 us
    psum x1, blocking collectives, local(): totals, picked = lax.psum((totals * jnp.exp(maxima - top), picked), 'grp')  45.1 us
    all_gather x1, blocking collectives, local(): lax.all_gather(views, 'grp', axis=0, tiled=True)  28.2 us
    unnamed x1, blocking collectives  19 us
  transfers between devices with their start and end apart: 3, of which 3 were waited for; matrix products, arithmetic and copies ran while one was open for 1% of the time, Pallas kernels for 0%

commit v1 on v0

v1 whole, which is shorter than its diff:
```python
import jax
import jax.numpy as jnp
from jax import lax
from jax.sharding import Mesh, PartitionSpec as P

inverse_softness = 10.0
very_low = -1e30
shard = 16

NAMES = ("zh", "x", "y", "zl", "core")
PLANE = ("x", "y")
LINE = ("zh", "zl")


def local(views, partner):
    zh, x, y, zl, core = (lax.axis_index(n) for n in NAMES)
    width = views.shape[1]
    digits = jnp.stack([partner // 128, partner % 128], axis=1).astype(jnp.bfloat16)
    packed = jnp.concatenate([views, jnp.pad(digits, ((0, 0), (0, 126)))], axis=1)
    spread = jnp.broadcast_to(packed[None], (16, shard, width + 128))
    rows = lax.all_to_all(spread, PLANE, 0, 0)
    row_views = rows[:, :, :width].reshape(256, width)
    rows_partner = (
        rows[:, :, width].astype(jnp.int32) * 128 + rows[:, :, width + 1].astype(jnp.int32)
    ).reshape(256)
    line = lax.all_gather(views, LINE, axis=0, tiled=True)
    column_views = lax.all_gather(line, "core", axis=0, tiled=True)

    r = jnp.arange(256, dtype=jnp.int32)
    row_ids = ((zh * 16 + r // 16) * 16 + zl * 2 + core) * 16 + r % 16
    c = jnp.arange(512, dtype=jnp.int32)
    column_ids = ((c // 128 % 2 * 16 + x * 4 + y) * 16 + c // 16 % 8 * 2 + c // 256) * 16 + c % 16

    scores = inverse_softness * jnp.dot(
        row_views, column_views.T, preferred_element_type=jnp.float32
    )
    positive = column_ids[None, :] == rows_partner[:, None]
    masked = jnp.where(row_ids[:, None] == column_ids[None, :], very_low, scores)
    picked = jnp.sum(jnp.where(positive, scores, 0.0), axis=1)
    row_top = jnp.max(masked, axis=1)
    row_part = row_top + jnp.log(jnp.sum(jnp.exp(masked - row_top[:, None]), axis=1))
    column_top = jnp.max(masked, axis=0)
    column_part = column_top + jnp.log(jnp.sum(jnp.exp(masked - column_top[None, :]), axis=0))

    row_stats = lax.all_to_all(
        jnp.broadcast_to(jnp.stack([row_part, picked])[None], (16, 2, 256)), PLANE, 0, 0
    )
    column_stats = lax.all_to_all(
        jnp.broadcast_to(column_part.reshape(1, 4, 128), (32, 4, 128)), LINE + ("core",), 0, 0
    ).reshape(32, 512)
    row_lse = jax.nn.logsumexp(row_stats[:, 0], axis=0)
    column_lse = jax.nn.logsumexp(column_stats, axis=0)
    loss = row_lse - jnp.sum(row_stats[:, 1], axis=0)
    view_loss = lax.dynamic_slice_in_dim(loss, (x * 4 + y) * shard, shard, 0)

    weight = (
        jnp.exp(masked - row_lse[:, None])
        + jnp.exp(masked - column_lse[None, :])
        - 2.0 * positive.astype(jnp.float32)
    ).astype(jnp.bfloat16)
    term = inverse_softness * jnp.dot(weight, column_views, preferred_element_type=jnp.float32)
    parts = lax.all_to_all(term.astype(jnp.bfloat16).reshape(16, shard, width), PLANE, 0, 0)
    derivative = jnp.sum(parts.astype(jnp.float32), axis=0).astype(jnp.bfloat16)
    return view_loss, derivative


def solution(mesh):
    split = Mesh(mesh.devices.reshape(2, 4, 4, 8, 2), NAMES)
    in_specs = (P(NAMES, None), P(NAMES))
    out_specs = (P(NAMES), P(NAMES, None))
    return jax.shard_map(
        local, mesh=split, in_specs=in_specs, out_specs=out_specs, check_vma=False
    )
```

time: 636 us -> 132 us (0.21)
  the two profiles are of different devices: /device:TPU:30 before, /device:TPU:8 now
where the time goes in v1:
time: 132 us; the launch traced here: 131 us
  blocking collectives  40.8 us (31%)
  waiting for transfers between devices  38.7 us (29%)
  starting transfers between devices  29 us (22%)
  between operations  14.1 us (11%)
  local copies, waits for them, and re-layouts  3.58 us (3%)
  matrix products  3.21 us (2%)
  other arithmetic  1.78 us (1%)
    all_gather x1, blocking collectives, local(): line = lax.all_gather(views, LINE, axis=0, tiled=True)  40.8 us
    all_to_all x1, waiting for transfers between devices, local(): lax.all_to_all(jnp.broadcast_to(column_part.reshape(1, 4, 128), (32, 4, 1...  14.3 us
    all_to_all x1, starting transfers between devices, local(): lax.all_to_all(jnp.broadcast_to(column_part.reshape(1, 4, 128), (32, 4, 1...  12 us
    all_to_all x1, waiting for transfers between devices, local(): rows = lax.all_to_all(spread, PLANE, 0, 0)  9.06 us
    all_to_all x1, waiting for transfers between devices, local(): lax.all_to_all(term.astype(jnp.bfloat16).reshape(16, shard, width), PLANE...  9.01 us
    all_to_all x1, starting transfers between devices, local(): rows = lax.all_to_all(spread, PLANE, 0, 0)  7.39 us
    all_to_all x1, waiting for transfers between devices, local(): lax.all_to_all(jnp.broadcast_to(jnp.stack([row_part, picked])[None], (16,...  6.25 us
    all_to_all x1, starting transfers between devices, local(): lax.all_to_all(term.astype(jnp.bfloat16).reshape(16, shard, width), PLANE...  4.82 us
  transfers between devices with their start and end apart: 5, of which 4 were waited for; matrix products, arithmetic and copies ran while one was open for 2% of the time, Pallas kernels for 0%

profile of v1, /device:TPU:8, one launch (start us, length us, event | category | flops | bytes accessed | tf_op | source)
XLA Modules:
  0.0 131.2 jit_solution(526677104023377040)
XLA Ops:
  7.2 0.0 all-gather.2.cloned.1.call-start
  7.2 40.8 %all_gather.6 = bf16[256,1024]{1,0:T(8,128)(2,1)} all-gather(bf16[16,1024]{1,0:T(8,128)(2,1)} %param.2), channel_id=1, replica_groups=mesh['zh'=2,'x'=4,'y'=4,'zl'=8,'core'=2] {'zh','zl'}, dimensions={0}, use_global_device_ids=true | all-gather | bytes 557056 | tf_op jit(solution)/shard_map/all_gather | solution.py:26
  48.0 0.0 copy-start.2
  48.0 0.0 copy-start
  48.0 0.0 all-gather.2.cloned.1.call-update
  48.0 0.6 copy-done.2
  48.7 0.1 copy.19
  48.8 0.0 copy-done
  48.8 0.9 broadcast_in_dim.21
  49.7 7.4 %all-to-all-start = ((bf16[16,16,1152]{2,1,0:T(8,128)(2,1)}), bf16[16,16,1152]{2,1,0:T(8,128)(2,1)S(1)}, u32[]{:S(2)}, u32[]{:S(2)}) async-start(bf16[16,16,1152]{2,1,0:T(8,128)(2,1)} %broadcast_in_dim.21), calls=%async_computation | async-start | bytes 1179648 | tf_op jit(solution)/shard_map/all_to_all | solution.py:21
  57.1 9.1 %all-to-all-done = bf16[16,16,1152]{2,1,0:T(8,128)(2,1)S(1)} async-done(((bf16[16,16,1152]{2,1,0:T(8,128)(2,1)}), bf16[16,16,1152]{2,1,0:T(8,128)(2,1)S(1)}, u32[]{:S(2)}, u32[]{:S(2)}) %all-to-all-start) | async-done | bytes 589856 | tf_op jit(solution)/shard_map/all_to_all | solution.py:21
  66.2 0.4 add_reduce_fusion
  66.6 0.1 add.221
  66.7 0.1 slice.20
  66.7 0.0 all-gather.2.cloned.1.call-done
  66.8 1.8 %fusion.4 = (f32[512]{0:T(512)S(1)}, f32[256]{0:T(256)S(1)}, f32[256,512]{1,0:T(8,128)S(1)}) fusion(s32[512]{0:T(512)S(1)} %fusion.29, s32[256]{0:T(256)S(1)} %fusion.41, bf16[256,1024]{1,0:T(8,128)(2,1)S(1)} %bitcast.23, bf16[512,1024]{1,0:T(8,128)(2,1)} %all-gather.2.cloned.1.call-done), kind=kOutput, calls=%fused_computation.11 | convolution fusion | flops 269090048 | bytes 2103296 | tf_op jit(solution)/shard_map/dot_general | solution.py:34
  68.6 0.0 copy-start.1
  68.6 0.4 exponential_reduce_fusion
  69.0 0.6 broadcast_in_dim.23
  69.6 4.8 %all-to-all-start.1 = ((f32[16,2,256]{2,1,0:T(2,128)}), f32[16,2,256]{2,1,0:T(2,128)S(1)}, u32[]{:S(2)}, u32[]{:S(2)}) async-start(f32[16,2,256]{2,1,0:T(2,128)} %broadcast_in_dim.23), calls=%async_computation.1 | async-start | bytes 65536 | tf_op jit(solution)/shard_map/all_to_all | solution.py:45
  74.4 6.3 %all-to-all-done.1 = f32[16,2,256]{2,1,0:T(2,128)S(1)} async-done(((f32[16,2,256]{2,1,0:T(2,128)}), f32[16,2,256]{2,1,0:T(2,128)S(1)}, u32[]{:S(2)}, u32[]{:S(2)}) %all-to-all-start.1) | async-done | bytes 32800 | tf_op jit(solution)/shard_map/all_to_all | solution.py:45
  80.7 0.6 broadcast_in_dim.25
  81.3 12.0 %all-to-all-start.2 = ((f32[32,4,128]{2,1,0:T(4,128)}), f32[32,4,128]{2,1,0:T(4,128)S(1)}, u32[]{:S(2)}, u32[]{:S(2)}) async-start(f32[32,4,128]{2,1,0:T(4,128)} %broadcast_in_dim.25), calls=%async_computation.2 | async-start | bytes 131072 | tf_op jit(solution)/shard_map/all_to_all | solution.py:48
  93.3 0.1 slice_reduce_fusion
  93.4 14.3 %all-to-all-done.2 = f32[32,4,128]{2,1,0:T(4,128)S(1)} async-done(((f32[32,4,128]{2,1,0:T(4,128)}), f32[32,4,128]{2,1,0:T(4,128)S(1)}, u32[]{:S(2)}, u32[]{:S(2)}) %all-to-all-start.2) | async-done | bytes 65568 | tf_op jit(solution)/shard_map/all_to_all | solution.py:48
  107.8 0.1 exponential_reduce_fusion.2
  107.8 0.0 copy-done.1
  107.8 1.4 %fusion = bf16[256,1024]{1,0:T(8,128)(2,1)} fusion(bf16[512,1024]{1,0:T(8,128)(2,1)S(1)} %copy-done.1, f32[256,512]{1,0:T(8,128)S(1)} %get-tuple-element.14, f32[512]{0:T(512)S(1)} %fusion.35, f32[256]{0:T(256)S(1)} %get-tuple-element.10, s32[512]{0:T(512)S(1)} %fusion.29, s32[256]{0:T(256)S(1)} %add.221, s32[256]{0:T(256)S(1)} %fusion.41), kind=kOutput, calls=%fused_computation.1 | convolution fusion | flops 270139392 | bytes 2104320 | tf_op jit(solution)/shard_map/dot_general | solution.py:61
  109.2 4.8 %all-to-all-start.3 = ((bf16[16,16,1024]{2,1,0:T(8,128)(2,1)}), bf16[16,16,1024]{2,1,0:T(8,128)(2,1)S(1)}, u32[]{:S(2)}, u32[]{:S(2)}) async-start(bf16[16,16,1024]{2,1,0:T(8,128)(2,1)} %bitcast.8), calls=%async_computation.3 | async-start | bytes 1048576 | tf_op jit(solution)/shard_map/all_to_all | solution.py:62
  114.1 0.6 dynamic_slice.3
  114.6 9.0 %all-to-all-done.3 = bf16[16,16,1024]{2,1,0:T(8,128)(2,1)S(1)} async-done(((bf16[16,16,1024]{2,1,0:T(8,128)(2,1)}), bf16[16,16,1024]{2,1,0:T(8,128)(2,1)S(1)}, u32[]{:S(2)}, u32[]{:S(2)}) %all-to-all-start.3) | async-done | bytes 524320 | tf_op jit(solution)/shard_map/all_to_all | solution.py:62
  123.7 0.7 reduce_sum.72
  (14 shorter events, 0.2 us)
Async XLA Ops:
  7.2 59.6 %all-gather.2.cloned.1.call-start = ((), (), s32[]{:S(2)}) async-start(), calls=%async_computation.4 | async-start | bytes 1572864 | tf_op jit(solution)/shard_map/all_gather | solution.py:27
  48.0 0.7 copy-start.2
  48.0 0.8 copy-start
  49.7 16.5 %all-to-all-start = ((bf16[16,16,1152]{2,1,0:T(8,128)(2,1)}), bf16[16,16,1152]{2,1,0:T(8,128)(2,1)S(1)}, u32[]{:S(2)}, u32[]{:S(2)}) async-start(bf16[16,16,1152]{2,1,0:T(8,128)(2,1)} %broadcast_in_dim.21), calls=%async_computation | async-start | bytes 1179648 | tf_op jit(solution)/shard_map/all_to_all | solution.py:21
  68.6 39.3 %copy-start.1 = (bf16[512,1024]{1,0:T(8,128)(2,1)S(1)}, bf16[512,1024]{1,0:T(8,128)(2,1)}, u32[]{:S(2)}) copy-start(bf16[512,1024]{1,0:T(8,128)(2,1)} %all-gather.2.cloned.1.call-done) | copy-start | bytes 3145732
  69.6 11.1 %all-to-all-start.1 = ((f32[16,2,256]{2,1,0:T(2,128)}), f32[16,2,256]{2,1,0:T(2,128)S(1)}, u32[]{:S(2)}, u32[]{:S(2)}) async-start(f32[16,2,256]{2,1,0:T(2,128)} %broadcast_in_dim.23), calls=%async_computation.1 | async-start | bytes 65536 | tf_op jit(solution)/shard_map/all_to_all | solution.py:45
  81.3 26.4 %all-to-all-start.2 = ((f32[32,4,128]{2,1,0:T(4,128)}), f32[32,4,128]{2,1,0:T(4,128)S(1)}, u32[]{:S(2)}, u32[]{:S(2)}) async-start(f32[32,4,128]{2,1,0:T(4,128)} %broadcast_in_dim.25), calls=%async_computation.2 | async-start | bytes 131072 | tf_op jit(solution)/shard_map/all_to_all | solution.py:48
  109.2 14.4 %all-to-all-start.3 = ((bf16[16,16,1024]{2,1,0:T(8,128)(2,1)}), bf16[16,16,1024]{2,1,0:T(8,128)(2,1)S(1)}, u32[]{:S(2)}, u32[]{:S(2)}) async-start(bf16[16,16,1024]{2,1,0:T(8,128)(2,1)} %bitcast.8), calls=%async_computation.3 | async-start | bytes 1048576 | tf_op jit(solution)/shard_map/all_to_all | solution.py:62
Sparse Core Ops, SparseCore 0:
  48.2 15.5 all-gather.1

commit v2 on v1

--- a/solution.py
+++ b/solution.py
@@ -17,19 +17,21 @@
     width = views.shape[1]
     digits = jnp.stack([partner // 128, partner % 128], axis=1).astype(jnp.bfloat16)
     packed = jnp.concatenate([views, jnp.pad(digits, ((0, 0), (0, 126)))], axis=1)
-    spread = jnp.broadcast_to(packed[None], (16, shard, width + 128))
-    rows = lax.all_to_all(spread, PLANE, 0, 0)
-    row_views = rows[:, :, :width].reshape(256, width)
-    rows_partner = (
-        rows[:, :, width].astype(jnp.int32) * 128 + rows[:, :, width + 1].astype(jnp.int32)
-    ).reshape(256)
-    line = lax.all_gather(views, LINE, axis=0, tiled=True)
-    column_views = lax.all_gather(line, "core", axis=0, tiled=True)
+    line = lax.all_to_all(jnp.broadcast_to(views[None], (16, shard, width)), LINE, 0, 0)
+    rows = lax.all_gather(packed, PLANE, axis=0, tiled=True)
+    line, rows = lax.optimization_barrier((line.reshape(256, width), rows))
+    row_views = rows[:, :width]
+    rows_partner = rows[:, width].astype(jnp.int32) * 128 + rows[:, width + 1].astype(jnp.int32)
+    other = lax.ppermute(line, "core", [(0, 1), (1, 0)])
+    column_views = jnp.concatenate([line, other])
+
+    def swap(per_column):
+        return jnp.where(core == 0, per_column, jnp.roll(per_column, 256))
 
     r = jnp.arange(256, dtype=jnp.int32)
     row_ids = ((zh * 16 + r // 16) * 16 + zl * 2 + core) * 16 + r % 16
     c = jnp.arange(512, dtype=jnp.int32)
-    column_ids = ((c // 128 % 2 * 16 + x * 4 + y) * 16 + c // 16 % 8 * 2 + c // 256) * 16 + c % 16
+    column_ids = ((c // 128 % 2 * 16 + x * 4 + y) * 16 + c // 16 % 8 * 2 + (core ^ (c // 256))) * 16 + c % 16
 
     scores = inverse_softness * jnp.dot(
         row_views, column_views.T, preferred_element_type=jnp.float32
@@ -46,10 +48,10 @@
         jnp.broadcast_to(jnp.stack([row_part, picked])[None], (16, 2, 256)), PLANE, 0, 0
     )
     column_stats = lax.all_to_all(
-        jnp.broadcast_to(column_part.reshape(1, 4, 128), (32, 4, 128)), LINE + ("core",), 0, 0
+        jnp.broadcast_to(swap(column_part).reshape(1, 4, 128), (32, 4, 128)), LINE + ("core",), 0, 0
     ).reshape(32, 512)
     row_lse = jax.nn.logsumexp(row_stats[:, 0], axis=0)
-    column_lse = jax.nn.logsumexp(column_stats, axis=0)
+    column_lse = swap(jax.nn.logsumexp(column_stats, axis=0))
     loss = row_lse - jnp.sum(row_stats[:, 1], axis=0)
     view_loss = lax.dynamic_slice_in_dim(loss, (x * 4 + y) * shard, shard, 0)
 

time: 132 us -> 105 us (0.80)
  blocking collectives: 40.8 us -> 24.1 us
  between operations: 14.1 us -> 0.77 us
  starting transfers between devices: 29 us -> 36 us
  waiting for transfers between devices: 38.7 us -> 36 us
    all_gather x1, blocking collectives: 40.8 us -> 24.1 us  [local(): rows = lax.all_gather(packed, PLANE, axis=0, tiled=True)]
    all_to_all x2, waiting for transfers between devices: 23.4 us -> 19.2 us  [the longest x1 14.3 us: local(): lax.all_to_all(jnp.broadcast_to(swap(column_part).reshape(1, 4, 128), (32...]
    all_to_all x1, starting transfers between devices: 4.82 us -> 7.39 us  [local(): lax.all_to_all(jnp.broadcast_to(jnp.stack([row_part, picked])[None], (16,...]
    all_to_all x2, starting transfers between devices: 19.4 us -> 21.9 us  [the longest x1 15.3 us: local(): lax.all_to_all(jnp.broadcast_to(views[None], (16, shard, width)), LINE, 0...]
    ppermute x0 -> x1, starting transfers between devices: none -> 1.91 us  [local(): other = lax.ppermute(line, 'core', [(0, 1), (1, 0)])]
    ppermute x0 -> x1, waiting for transfers between devices: none -> 1.6 us  [local(): other = lax.ppermute(line, 'core', [(0, 1), (1, 0)])]
  transfers between devices with their start and end apart: 5 -> 5, of which waited for: 4 -> 5; matrix products, arithmetic and copies ran while one was open for 2% -> 1% of each run, Pallas kernels for 0% -> 0%
where the time goes in v2:
time: 105 us; the launch traced here: 104 us
  starting transfers between devices  36 us (34%)
  waiting for transfers between devices  36 us (34%)
  blocking collectives  24.1 us (23%)
  local copies, waits for them, and re-layouts  3.63 us (3%)
  matrix products  1.99 us (2%)
  other arithmetic  1.56 us (1%)
    all_gather x1, blocking collectives, local(): rows = lax.all_gather(packed, PLANE, axis=0, tiled=True)  24.1 us
    all_to_all x1, starting transfers between devices, local(): lax.all_to_all(jnp.broadcast_to(views[None], (16, shard, width)), LINE, 0...  15.3 us
    all_to_all x1, waiting for transfers between devices, local(): lax.all_to_all(jnp.broadcast_to(swap(column_part).reshape(1, 4, 128), (32...  14.3 us
    all_to_all x1, waiting for transfers between devices, local(): lax.all_to_all(term.astype(jnp.bfloat16).reshape(16, shard, width), PLANE...  9.01 us
    all_to_all x1, starting transfers between devices, local(): lax.all_to_all(jnp.broadcast_to(jnp.stack([row_part, picked])[None], (16,...  7.39 us
    all_to_all x1, starting transfers between devices, local(): lax.all_to_all(jnp.broadcast_to(swap(column_part).reshape(1, 4, 128), (32...  6.58 us
    all_to_all x1, waiting for transfers between devices, local(): lax.all_to_all(jnp.broadcast_to(jnp.stack([row_part, picked])[None], (16,...  6.25 us
    all_to_all x1, waiting for transfers between devices, local(): lax.all_to_all(jnp.broadcast_to(views[None], (16, shard, width)), LINE, 0...  4.87 us
  transfers between devices with their start and end apart: 5, of which 5 were waited for; matrix products, arithmetic and copies ran while one was open for 1% of the time, Pallas kernels for 0%

profile of v2, /device:TPU:8, one launch (start us, length us, event | category | flops | bytes accessed | tf_op | source)
XLA Modules:
  0.0 104.1 jit_solution(9822304248063729977)
XLA Ops:
  0.6 1.6 %broadcast_in_dim.21 = bf16[16,16,1024]{2,1,0:T(8,128)(2,1)} broadcast(bf16[16,1024]{1,0:T(8,128)(2,1)} %param.2), dimensions={1,2} | broadcast | bytes 557056 | tf_op jit(solution)/shard_map/broadcast_in_dim | solution.py:20
  2.2 0.0 copy-start.1
  2.2 0.0 copy-start
  2.2 15.3 %all-to-all-start = ((bf16[16,16,1024]{2,1,0:T(8,128)(2,1)}), bf16[16,16,1024]{2,1,0:T(8,128)(2,1)S(1)}, u32[]{:S(2)}, u32[]{:S(2)}) async-start(bf16[16,16,1024]{2,1,0:T(8,128)(2,1)} %broadcast_in_dim.21), calls=%async_computation | async-start | bytes 1048576 | tf_op jit(solution)/shard_map/all_to_all | solution.py:20
  17.6 0.0 copy-done.1
  17.6 0.1 copy.17
  17.7 0.0 copy-done
  17.7 24.1 %all_gather.3 = bf16[256,1152]{1,0:T(8,128)(2,1)S(1)} all-gather(bf16[16,1152]{1,0:T(8,128)(2,1)S(1)} %fusion.17), channel_id=1, replica_groups=mesh['zh'=2,'x'=4,'y'=4,'zl'=8,'core'=2] {'x','y'}, dimensions={0}, use_global_device_ids=true | all-gather | bytes 626688 | tf_op jit(solution)/shard_map/all_gather | solution.py:21
  41.8 4.9 %all-to-all-done = bf16[16,16,1024]{2,1,0:T(8,128)(2,1)S(1)} async-done(((bf16[16,16,1024]{2,1,0:T(8,128)(2,1)}), bf16[16,16,1024]{2,1,0:T(8,128)(2,1)S(1)}, u32[]{:S(2)}, u32[]{:S(2)}) %all-to-all-start) | async-done | bytes 524320 | tf_op jit(solution)/shard_map/all_to_all | solution.py:20
  46.7 1.9 %collective-permute-start = (bf16[256,1024]{1,0:T(8,128)(2,1)S(1)}, bf16[256,1024]{1,0:T(8,128)(2,1)S(1)}, u32[]{:S(2)}, u32[]{:S(2)}) collective-permute-start(bf16[256,1024]{1,0:T(8,128)(2,1)S(1)} %bitcast.26), channel_id=1, source_target_pairs={{0,1},{1,0},{2,3},{3,2},{4,5},{5,4},{6,7},{7,6},{8,9},{9,8},{10,11... | collective-permute-start | bytes 1572872 | tf_op jit(solution)/shard_map/ppermute | solution.py:25
  48.6 0.2 add_reduce_fusion
  48.9 1.6 %collective-permute-done = bf16[256,1024]{1,0:T(8,128)(2,1)S(1)} collective-permute-done((bf16[256,1024]{1,0:T(8,128)(2,1)S(1)}, bf16[256,1024]{1,0:T(8,128)(2,1)S(1)}, u32[]{:S(2)}, u32[]{:S(2)}) %collective-permute-start) | collective-permute-done | bytes 524320 | tf_op jit(solution)/shard_map/ppermute | solution.py:25
  50.5 0.6 fusion.5
  51.1 0.4 exponential_reduce_fusion
  51.5 0.6 broadcast_in_dim.23
  52.1 7.4 %all-to-all-start.1 = ((f32[16,2,256]{2,1,0:T(2,128)}), f32[16,2,256]{2,1,0:T(2,128)S(1)}, u32[]{:S(2)}, u32[]{:S(2)}) async-start(f32[16,2,256]{2,1,0:T(2,128)} %broadcast_in_dim.23), calls=%async_computation.1 | async-start | bytes 65536 | tf_op jit(solution)/shard_map/all_to_all | solution.py:47
  59.5 6.2 %all-to-all-done.1 = f32[16,2,256]{2,1,0:T(2,128)S(1)} async-done(((f32[16,2,256]{2,1,0:T(2,128)}), f32[16,2,256]{2,1,0:T(2,128)S(1)}, u32[]{:S(2)}, u32[]{:S(2)}) %all-to-all-start.1) | async-done | bytes 32800 | tf_op jit(solution)/shard_map/all_to_all | solution.py:47
  65.8 0.6 broadcast_in_dim.25
  66.4 6.6 %all-to-all-start.2 = ((f32[32,4,128]{2,1,0:T(4,128)}), f32[32,4,128]{2,1,0:T(4,128)S(1)}, u32[]{:S(2)}, u32[]{:S(2)}) async-start(f32[32,4,128]{2,1,0:T(4,128)} %broadcast_in_dim.25), calls=%async_computation.2 | async-start | bytes 131072 | tf_op jit(solution)/shard_map/all_to_all | solution.py:50
  73.0 0.1 slice_reduce_fusion
  73.1 14.3 %all-to-all-done.2 = f32[32,4,128]{2,1,0:T(4,128)S(1)} async-done(((f32[32,4,128]{2,1,0:T(4,128)}), f32[32,4,128]{2,1,0:T(4,128)S(1)}, u32[]{:S(2)}, u32[]{:S(2)}) %all-to-all-start.2) | async-done | bytes 65568 | tf_op jit(solution)/shard_map/all_to_all | solution.py:50
  87.5 0.1 exponential_reduce_fusion.2
  87.6 1.4 %fusion = bf16[256,1024]{1,0:T(8,128)(2,1)} fusion(bf16[512,1024]{1,0:T(8,128)(2,1)S(1)} %constant_dynamic-update-slice_fusion, f32[256,512]{1,0:T(8,128)S(1)} %get-tuple-element.22, f32[512]{0:T(512)S(1)} %maximum_select_fusion.1, f32[256]{0:T(256)S(1)} %get-tuple-element.14, s32[512]{0:T(512)S(1)} %fusion.30, s32[256]{0:T(256)S(1)} %add_reduce_fusion, ...), kind=kOutput, calls=%fused_computation.1 | convolution fusion | flops 270139392 | bytes 2104320 | tf_op jit(solution)/shard_map/dot_general | solution.py:63
  89.0 4.8 %all-to-all-start.3 = ((bf16[16,16,1024]{2,1,0:T(8,128)(2,1)}), bf16[16,16,1024]{2,1,0:T(8,128)(2,1)S(1)}, u32[]{:S(2)}, u32[]{:S(2)}) async-start(bf16[16,16,1024]{2,1,0:T(8,128)(2,1)} %bitcast.10), calls=%async_computation.3 | async-start | bytes 1048576 | tf_op jit(solution)/shard_map/all_to_all | solution.py:64
  93.8 0.6 dynamic_slice.3
  94.4 9.0 %all-to-all-done.3 = bf16[16,16,1024]{2,1,0:T(8,128)(2,1)S(1)} async-done(((bf16[16,16,1024]{2,1,0:T(8,128)(2,1)}), bf16[16,16,1024]{2,1,0:T(8,128)(2,1)S(1)}, u32[]{:S(2)}, u32[]{:S(2)}) %all-to-all-start.3) | async-done | bytes 524320 | tf_op jit(solution)/shard_map/all_to_all | solution.py:64
  103.4 0.7 reduce_sum.72
  (20 shorter events, 0.3 us)
Async XLA Ops:
  2.2 15.3 %copy-start.1 = (s32[16]{0:T(128)S(1)}, s32[16]{0:T(128)}, u32[]{:S(2)}) copy-start(s32[16]{0:T(128)} %param.3) | copy-start | bytes 196
  2.2 15.5 %copy-start = (bf16[16,1024]{1,0:T(8,128)(2,1)S(1)}, bf16[16,1024]{1,0:T(8,128)(2,1)}, u32[]{:S(2)}) copy-start(bf16[16,1024]{1,0:T(8,128)(2,1)} %param.2) | copy-start | bytes 98308
  2.2 44.4 %all-to-all-start = ((bf16[16,16,1024]{2,1,0:T(8,128)(2,1)}), bf16[16,16,1024]{2,1,0:T(8,128)(2,1)S(1)}, u32[]{:S(2)}, u32[]{:S(2)}) async-start(bf16[16,16,1024]{2,1,0:T(8,128)(2,1)} %broadcast_in_dim.21), calls=%async_computation | async-start | bytes 1048576 | tf_op jit(solution)/shard_map/all_to_all | solution.py:20
  46.7 3.8 %collective-permute-start = (bf16[256,1024]{1,0:T(8,128)(2,1)S(1)}, bf16[256,1024]{1,0:T(8,128)(2,1)S(1)}, u32[]{:S(2)}, u32[]{:S(2)}) collective-permute-start(bf16[256,1024]{1,0:T(8,128)(2,1)S(1)} %bitcast.26), channel_id=1, source_target_pairs={{0,1},{1,0},{2,3},{3,2},{4,5},{5,4},{6,7},{7,6},{8,9},{9,8},{10,11... | collective-permute-start | bytes 1572872 | tf_op jit(solution)/shard_map/ppermute | solution.py:25
  52.1 13.6 %all-to-all-start.1 = ((f32[16,2,256]{2,1,0:T(2,128)}), f32[16,2,256]{2,1,0:T(2,128)S(1)}, u32[]{:S(2)}, u32[]{:S(2)}) async-start(f32[16,2,256]{2,1,0:T(2,128)} %broadcast_in_dim.23), calls=%async_computation.1 | async-start | bytes 65536 | tf_op jit(solution)/shard_map/all_to_all | solution.py:47
  66.4 21.0 %all-to-all-start.2 = ((f32[32,4,128]{2,1,0:T(4,128)}), f32[32,4,128]{2,1,0:T(4,128)S(1)}, u32[]{:S(2)}, u32[]{:S(2)}) async-start(f32[32,4,128]{2,1,0:T(4,128)} %broadcast_in_dim.25), calls=%async_computation.2 | async-start | bytes 131072 | tf_op jit(solution)/shard_map/all_to_all | solution.py:50
  89.0 14.4 %all-to-all-start.3 = ((bf16[16,16,1024]{2,1,0:T(8,128)(2,1)}), bf16[16,16,1024]{2,1,0:T(8,128)(2,1)S(1)}, u32[]{:S(2)}, u32[]{:S(2)}) async-start(bf16[16,16,1024]{2,1,0:T(8,128)(2,1)} %bitcast.10), calls=%async_computation.3 | async-start | bytes 1048576 | tf_op jit(solution)/shard_map/all_to_all | solution.py:64

commit v3 on v2

--- a/solution.py
+++ b/solution.py
@@ -44,12 +44,13 @@
     column_top = jnp.max(masked, axis=0)
     column_part = column_top + jnp.log(jnp.sum(jnp.exp(masked - column_top[None, :]), axis=0))
 
-    row_stats = lax.all_to_all(
-        jnp.broadcast_to(jnp.stack([row_part, picked])[None], (16, 2, 256)), PLANE, 0, 0
-    )
-    column_stats = lax.all_to_all(
-        jnp.broadcast_to(swap(column_part).reshape(1, 4, 128), (32, 4, 128)), LINE + ("core",), 0, 0
-    ).reshape(32, 512)
+    row_out = jnp.broadcast_to(jnp.stack([row_part, picked])[None], (16, 2, 256))
+    column_out = jnp.broadcast_to(swap(column_part).reshape(1, 4, 128), (32, 4, 128))
+    row_out, column_out = lax.optimization_barrier((row_out, column_out))
+    row_stats = lax.all_gather(row_out[0], PLANE)
+    column_stats = lax.all_to_all(column_out, LINE + ("core",), 0, 0)
+    row_stats, column_stats = lax.optimization_barrier((row_stats, column_stats))
+    column_stats = column_stats.reshape(32, 512)
     row_lse = jax.nn.logsumexp(row_stats[:, 0], axis=0)
     column_lse = swap(jax.nn.logsumexp(column_stats, axis=0))
     loss = row_lse - jnp.sum(row_stats[:, 1], axis=0)

time: 105 us -> 100 us (0.952)
  the two profiles are of different devices: /device:TPU:8 before, /device:TPU:32 now
where the time goes in v3:
time: 100 us; the launch traced here: 99.7 us
  blocking collectives  47 us (47%)
  starting transfers between devices  30.9 us (31%)
  waiting for transfers between devices  14.4 us (14%)
  local copies, waits for them, and re-layouts  3.02 us (3%)
  matrix products  1.99 us (2%)
  other arithmetic  1.56 us (2%)
    all_gather x1, blocking collectives, local(): rows = lax.all_gather(packed, PLANE, axis=0, tiled=True)  24.8 us
    all_gather x1, blocking collectives, local(): row_stats = lax.all_gather(row_out[0], PLANE)  22.2 us
    all_to_all x1, starting transfers between devices, local(): lax.all_to_all(jnp.broadcast_to(views[None], (16, shard, width)), LINE, 0...  15.3 us
    all_to_all x1, waiting for transfers between devices, local(): lax.all_to_all(term.astype(jnp.bfloat16).reshape(16, shard, width), PLANE...  9.5 us
    all_to_all x1, starting transfers between devices, local(): column_stats = lax.all_to_all(column_out, LINE + ('core',), 0, 0)  8.97 us
    all_to_all x1, starting transfers between devices, local(): lax.all_to_all(term.astype(jnp.bfloat16).reshape(16, shard, width), PLANE...  4.68 us
    all_to_all x1, waiting for transfers between devices, local(): lax.all_to_all(jnp.broadcast_to(views[None], (16, shard, width)), LINE, 0...  3.28 us
  transfers between devices with their start and end apart: 4, of which 3 were waited for; matrix products, arithmetic and copies ran while one was open for 1% of the time, Pallas kernels for 0%

profile of v3, /device:TPU:32, one launch (start us, length us, event | category | flops | bytes accessed | tf_op | source)
XLA Modules:
  0.0 99.7 jit_solution(9909858988090238627)
XLA Ops:
  0.6 1.6 %broadcast_in_dim.21 = bf16[16,16,1024]{2,1,0:T(8,128)(2,1)} broadcast(bf16[16,1024]{1,0:T(8,128)(2,1)} %param.2), dimensions={1,2} | broadcast | bytes 557056 | tf_op jit(solution)/shard_map/broadcast_in_dim | solution.py:20
  2.2 0.0 copy-start.1
  2.2 0.0 copy-start
  2.2 15.3 %all-to-all-start = ((bf16[16,16,1024]{2,1,0:T(8,128)(2,1)}), bf16[16,16,1024]{2,1,0:T(8,128)(2,1)S(1)}, u32[]{:S(2)}, u32[]{:S(2)}) async-start(bf16[16,16,1024]{2,1,0:T(8,128)(2,1)} %broadcast_in_dim.21), calls=%async_computation | async-start | bytes 1048576 | tf_op jit(solution)/shard_map/all_to_all | solution.py:20
  17.6 0.0 copy-done.1
  17.6 0.1 copy.12
  17.7 0.0 copy-done
  17.7 24.8 %all_gather.6 = bf16[256,1152]{1,0:T(8,128)(2,1)S(1)} all-gather(bf16[16,1152]{1,0:T(8,128)(2,1)S(1)} %fusion.17), channel_id=1, replica_groups=mesh['zh'=2,'x'=4,'y'=4,'zl'=8,'core'=2] {'x','y'}, dimensions={0}, use_global_device_ids=true | all-gather | bytes 626688 | tf_op jit(solution)/shard_map/all_gather | solution.py:21
  42.5 3.3 %all-to-all-done = bf16[16,16,1024]{2,1,0:T(8,128)(2,1)S(1)} async-done(((bf16[16,16,1024]{2,1,0:T(8,128)(2,1)}), bf16[16,16,1024]{2,1,0:T(8,128)(2,1)S(1)}, u32[]{:S(2)}, u32[]{:S(2)}) %all-to-all-start) | async-done | bytes 524320 | tf_op jit(solution)/shard_map/all_to_all | solution.py:20
  45.8 1.9 %collective-permute-start = (bf16[256,1024]{1,0:T(8,128)(2,1)S(1)}, bf16[256,1024]{1,0:T(8,128)(2,1)S(1)}, u32[]{:S(2)}, u32[]{:S(2)}) collective-permute-start(bf16[256,1024]{1,0:T(8,128)(2,1)S(1)} %bitcast.26), channel_id=1, source_target_pairs={{0,1},{1,0},{2,3},{3,2},{4,5},{5,4},{6,7},{7,6},{8,9},{9,8},{10,11... | collective-permute-start | bytes 1572872 | tf_op jit(solution)/shard_map/ppermute | solution.py:25
  47.8 0.2 add_reduce_fusion
  48.0 1.6 %collective-permute-done = bf16[256,1024]{1,0:T(8,128)(2,1)S(1)} collective-permute-done((bf16[256,1024]{1,0:T(8,128)(2,1)S(1)}, bf16[256,1024]{1,0:T(8,128)(2,1)S(1)}, u32[]{:S(2)}, u32[]{:S(2)}) %collective-permute-start) | collective-permute-done | bytes 524320 | tf_op jit(solution)/shard_map/ppermute | solution.py:25
  49.6 0.6 fusion.5
  50.2 0.4 exponential_reduce_fusion
  50.7 0.6 broadcast_in_dim.24
  51.3 9.0 %all-to-all-start.1 = ((f32[32,4,128]{2,1,0:T(4,128)}), f32[32,4,128]{2,1,0:T(4,128)S(1)}, u32[]{:S(2)}, u32[]{:S(2)}) async-start(f32[32,4,128]{2,1,0:T(4,128)} %broadcast_in_dim.24), calls=%async_computation.1 | async-start | bytes 131072 | tf_op jit(solution)/shard_map/all_to_all | solution.py:51
  60.3 22.2 %all_gather.7 = f32[16,2,256]{2,1,0:T(2,128)S(1)} all-gather(f32[1,2,256]{2,1,0:T(2,128)S(1)} %slice.51), channel_id=1, replica_groups=mesh['zh'=2,'x'=4,'y'=4,'zl'=8,'core'=2] {'x','y'}, dimensions={0}, use_global_device_ids=true | all-gather | bytes 34816 | tf_op jit(solution)/shard_map/all_gather | solution.py:50
  82.5 0.0 all-to-all-done.1
  82.6 0.1 exponential_reduce_fusion.2
  82.7 0.1 slice_reduce_fusion
  82.8 1.4 %fusion = bf16[256,1024]{1,0:T(8,128)(2,1)} fusion(bf16[512,1024]{1,0:T(8,128)(2,1)S(1)} %constant_dynamic-update-slice_fusion, f32[256,512]{1,0:T(8,128)S(1)} %get-tuple-element.30, f32[512]{0:T(512)S(1)} %maximum_select_fusion.1, f32[256]{0:T(256)S(1)} %get-tuple-element.22, s32[512]{0:T(512)S(1)} %fusion.30, s32[256]{0:T(256)S(1)} %add_reduce_fusion, ...), kind=kOutput, calls=%fused_computation.1 | convolution fusion | flops 270139392 | bytes 2104320 | tf_op jit(solution)/shard_map/dot_general | solution.py:64
  84.2 4.7 %all-to-all-start.2 = ((bf16[16,16,1024]{2,1,0:T(8,128)(2,1)}), bf16[16,16,1024]{2,1,0:T(8,128)(2,1)S(1)}, u32[]{:S(2)}, u32[]{:S(2)}) async-start(bf16[16,16,1024]{2,1,0:T(8,128)(2,1)} %bitcast.10), calls=%async_computation.2 | async-start | bytes 1048576 | tf_op jit(solution)/shard_map/all_to_all | solution.py:65
  88.9 0.6 dynamic_slice.3
  89.5 9.5 %all-to-all-done.2 = bf16[16,16,1024]{2,1,0:T(8,128)(2,1)S(1)} async-done(((bf16[16,16,1024]{2,1,0:T(8,128)(2,1)}), bf16[16,16,1024]{2,1,0:T(8,128)(2,1)S(1)}, u32[]{:S(2)}, u32[]{:S(2)}) %all-to-all-start.2) | async-done | bytes 524320 | tf_op jit(solution)/shard_map/all_to_all | solution.py:65
  99.0 0.7 reduce_sum.72
  (22 shorter events, 0.3 us)
Async XLA Ops:
  2.2 15.3 %copy-start.1 = (s32[16]{0:T(128)S(1)}, s32[16]{0:T(128)}, u32[]{:S(2)}) copy-start(s32[16]{0:T(128)} %param.3) | copy-start | bytes 196
  2.2 15.5 %copy-start = (bf16[16,1024]{1,0:T(8,128)(2,1)S(1)}, bf16[16,1024]{1,0:T(8,128)(2,1)}, u32[]{:S(2)}) copy-start(bf16[16,1024]{1,0:T(8,128)(2,1)} %param.2) | copy-start | bytes 98308
  2.2 43.6 %all-to-all-start = ((bf16[16,16,1024]{2,1,0:T(8,128)(2,1)}), bf16[16,16,1024]{2,1,0:T(8,128)(2,1)S(1)}, u32[]{:S(2)}, u32[]{:S(2)}) async-start(bf16[16,16,1024]{2,1,0:T(8,128)(2,1)} %broadcast_in_dim.21), calls=%async_computation | async-start | bytes 1048576 | tf_op jit(solution)/shard_map/all_to_all | solution.py:20
  45.8 3.8 %collective-permute-start = (bf16[256,1024]{1,0:T(8,128)(2,1)S(1)}, bf16[256,1024]{1,0:T(8,128)(2,1)S(1)}, u32[]{:S(2)}, u32[]{:S(2)}) collective-permute-start(bf16[256,1024]{1,0:T(8,128)(2,1)S(1)} %bitcast.26), channel_id=1, source_target_pairs={{0,1},{1,0},{2,3},{3,2},{4,5},{5,4},{6,7},{7,6},{8,9},{9,8},{10,11... | collective-permute-start | bytes 1572872 | tf_op jit(solution)/shard_map/ppermute | solution.py:25
  51.3 31.2 %all-to-all-start.1 = ((f32[32,4,128]{2,1,0:T(4,128)}), f32[32,4,128]{2,1,0:T(4,128)S(1)}, u32[]{:S(2)}, u32[]{:S(2)}) async-start(f32[32,4,128]{2,1,0:T(4,128)} %broadcast_in_dim.24), calls=%async_computation.1 | async-start | bytes 131072 | tf_op jit(solution)/shard_map/all_to_all | solution.py:51
  84.2 14.8 %all-to-all-start.2 = ((bf16[16,16,1024]{2,1,0:T(8,128)(2,1)}), bf16[16,16,1024]{2,1,0:T(8,128)(2,1)S(1)}, u32[]{:S(2)}, u32[]{:S(2)}) async-start(bf16[16,16,1024]{2,1,0:T(8,128)(2,1)} %bitcast.10), calls=%async_computation.2 | async-start | bytes 1048576 | tf_op jit(solution)/shard_map/all_to_all | solution.py:65

commit v4 on v3

--- a/solution.py
+++ b/solution.py
@@ -10,6 +10,10 @@
 NAMES = ("zh", "x", "y", "zl", "core")
 PLANE = ("x", "y")
 LINE = ("zh", "zl")
+
+
+def combine(stats):
+    return jnp.stack([jax.nn.logsumexp(stats[:, 0], axis=0), jnp.sum(stats[:, 1], axis=0)])
 
 
 def local(views, partner):
@@ -44,16 +48,15 @@
     column_top = jnp.max(masked, axis=0)
     column_part = column_top + jnp.log(jnp.sum(jnp.exp(masked - column_top[None, :]), axis=0))
 
-    row_out = jnp.broadcast_to(jnp.stack([row_part, picked])[None], (16, 2, 256))
     column_out = jnp.broadcast_to(swap(column_part).reshape(1, 4, 128), (32, 4, 128))
-    row_out, column_out = lax.optimization_barrier((row_out, column_out))
-    row_stats = lax.all_gather(row_out[0], PLANE)
+    row_stats = jnp.stack([row_part, picked])
     column_stats = lax.all_to_all(column_out, LINE + ("core",), 0, 0)
+    row_stats = combine(lax.all_gather(row_stats, "x"))
+    row_stats = lax.all_gather(row_stats, "y")
     row_stats, column_stats = lax.optimization_barrier((row_stats, column_stats))
-    column_stats = column_stats.reshape(32, 512)
-    row_lse = jax.nn.logsumexp(row_stats[:, 0], axis=0)
-    column_lse = swap(jax.nn.logsumexp(column_stats, axis=0))
-    loss = row_lse - jnp.sum(row_stats[:, 1], axis=0)
+    row_lse, picked = combine(row_stats)
+    column_lse = swap(jax.nn.logsumexp(column_stats.reshape(32, 512), axis=0))
+    loss = row_lse - picked
     view_loss = lax.dynamic_slice_in_dim(loss, (x * 4 + y) * shard, shard, 0)
 
     weight = (

time: 100 us -> 99.8 us (level)
  blocking collectives: 47 us -> 45.6 us
    all_gather x1 -> x2, blocking collectives: 22.2 us -> 20.8 us  [the longest x1 10.4 us: local(): row_stats = combine(lax.all_gather(row_stats, 'x'))]
where the time goes in v4:
time: 99.8 us; the launch traced here: 99.2 us
  blocking collectives  45.6 us (46%)
  starting transfers between devices  31.8 us (32%)
  waiting for transfers between devices  14.4 us (14%)
  local copies, waits for them, and re-layouts  3.01 us (3%)
  matrix products  1.98 us (2%)
  other arithmetic  1.61 us (2%)
    all_gather x1, blocking collectives, local(): rows = lax.all_gather(packed, PLANE, axis=0, tiled=True)  24.8 us
    all_to_all x1, starting transfers between devices, local(): lax.all_to_all(jnp.broadcast_to(views[None], (16, shard, width)), LINE, 0...  15.3 us
    all_gather x1, blocking collectives, local(): row_stats = combine(lax.all_gather(row_stats, 'x'))  10.4 us
    all_gather x1, blocking collectives, local(): row_stats = lax.all_gather(row_stats, 'y')  10.4 us
    all_to_all x1, waiting for transfers between devices, local(): lax.all_to_all(term.astype(jnp.bfloat16).reshape(16, shard, width), PLANE...  9.5 us
    all_to_all x1, starting transfers between devices, local(): column_stats = lax.all_to_all(column_out, LINE + ('core',), 0, 0)  8.96 us
    all_to_all x1, starting transfers between devices, local(): lax.all_to_all(term.astype(jnp.bfloat16).reshape(16, shard, width), PLANE...  5.63 us
    all_to_all x1, waiting for transfers between devices, local(): lax.all_to_all(jnp.broadcast_to(views[None], (16, shard, width)), LINE, 0...  3.28 us
  transfers between devices with their start and end apart: 4, of which 3 were waited for; matrix products, arithmetic and copies ran while one was open for 1% of the time, Pallas kernels for 0%

profile of v4, /device:TPU:32, one launch (start us, length us, event | category | flops | bytes accessed | tf_op | source)
XLA Modules:
  0.0 99.2 jit_solution(1454269393588629008)
XLA Ops:
  0.6 1.6 %broadcast_in_dim.17 = bf16[16,16,1024]{2,1,0:T(8,128)(2,1)} broadcast(bf16[16,1024]{1,0:T(8,128)(2,1)} %param.2), dimensions={1,2} | broadcast | bytes 557056 | tf_op jit(solution)/shard_map/broadcast_in_dim | solution.py:24
  2.2 0.0 copy-start.1
  2.2 0.0 copy-start
  2.2 15.3 %all-to-all-start = ((bf16[16,16,1024]{2,1,0:T(8,128)(2,1)}), bf16[16,16,1024]{2,1,0:T(8,128)(2,1)S(1)}, u32[]{:S(2)}, u32[]{:S(2)}) async-start(bf16[16,16,1024]{2,1,0:T(8,128)(2,1)} %broadcast_in_dim.17), calls=%async_computation | async-start | bytes 1048576 | tf_op jit(solution)/shard_map/all_to_all | solution.py:24
  17.6 0.0 copy-done.1
  17.6 0.1 copy.13
  17.7 0.0 copy-done
  17.7 24.8 %all_gather.15 = bf16[256,1152]{1,0:T(8,128)(2,1)S(1)} all-gather(bf16[16,1152]{1,0:T(8,128)(2,1)S(1)} %fusion.17), channel_id=1, replica_groups=mesh['zh'=2,'x'=4,'y'=4,'zl'=8,'core'=2] {'x','y'}, dimensions={0}, use_global_device_ids=true | all-gather | bytes 626688 | tf_op jit(solution)/shard_map/all_gather | solution.py:25
  42.5 3.3 %all-to-all-done = bf16[16,16,1024]{2,1,0:T(8,128)(2,1)S(1)} async-done(((bf16[16,16,1024]{2,1,0:T(8,128)(2,1)}), bf16[16,16,1024]{2,1,0:T(8,128)(2,1)S(1)}, u32[]{:S(2)}, u32[]{:S(2)}) %all-to-all-start) | async-done | bytes 524320 | tf_op jit(solution)/shard_map/all_to_all | solution.py:24
  45.8 1.9 %collective-permute-start = (bf16[256,1024]{1,0:T(8,128)(2,1)S(1)}, bf16[256,1024]{1,0:T(8,128)(2,1)S(1)}, u32[]{:S(2)}, u32[]{:S(2)}) collective-permute-start(bf16[256,1024]{1,0:T(8,128)(2,1)S(1)} %bitcast.39), channel_id=1, source_target_pairs={{0,1},{1,0},{2,3},{3,2},{4,5},{5,4},{6,7},{7,6},{8,9},{9,8},{10,11... | collective-permute-start | bytes 1572872 | tf_op jit(solution)/shard_map/ppermute | solution.py:29
  47.8 0.2 add_reduce_fusion
  48.0 1.6 %collective-permute-done = bf16[256,1024]{1,0:T(8,128)(2,1)S(1)} collective-permute-done((bf16[256,1024]{1,0:T(8,128)(2,1)S(1)}, bf16[256,1024]{1,0:T(8,128)(2,1)S(1)}, u32[]{:S(2)}, u32[]{:S(2)}) %collective-permute-start) | collective-permute-done | bytes 524320 | tf_op jit(solution)/shard_map/ppermute | solution.py:29
  49.6 0.6 fusion.5
  50.2 0.4 exponential_reduce_fusion
  50.6 0.6 broadcast_in_dim.19
  51.3 9.0 %all-to-all-start.1 = ((f32[32,4,128]{2,1,0:T(4,128)}), f32[32,4,128]{2,1,0:T(4,128)S(1)}, u32[]{:S(2)}, u32[]{:S(2)}) async-start(f32[32,4,128]{2,1,0:T(4,128)} %broadcast_in_dim.19), calls=%async_computation.1 | async-start | bytes 131072 | tf_op jit(solution)/shard_map/all_to_all | solution.py:53
  60.3 10.4 %all-gather.2 = f32[4,2,256]{2,1,0:T(2,128)S(1)} all-gather(f32[1,2,256]{2,1,0:T(2,128)S(1)} %maximum_bitcast_fusion), channel_id=2, replica_groups=mesh['zh'=2,'x'=4,'y'=4,'zl'=8,'core'=2] {'x'}, dimensions={0}, use_global_device_ids=true | all-gather | bytes 10240 | tf_op jit(solution)/shard_map/all_gather | solution.py:54
  70.8 10.4 %all-gather.3 = f32[4,2,256]{2,1,0:T(2,128)S(1)} all-gather(f32[1,2,256]{2,1,0:T(2,128)S(1)} %maximum_bitcast_fusion.1), channel_id=3, replica_groups=mesh['zh'=2,'x'=4,'y'=4,'zl'=8,'core'=2] {'y'}, dimensions={0}, use_global_device_ids=true | all-gather | bytes 10240 | tf_op jit(solution)/shard_map/all_gather | solution.py:55
  81.1 0.0 all-to-all-done.1
  81.2 0.1 exponential_reduce_fusion.2
  81.4 1.4 %fusion = bf16[256,1024]{1,0:T(8,128)(2,1)} fusion(bf16[512,1024]{1,0:T(8,128)(2,1)S(1)} %constant_dynamic-update-slice_fusion, f32[256,512]{1,0:T(8,128)S(1)} %get-tuple-element.29, f32[512]{0:T(512)S(1)} %maximum_select_fusion.1, f32[256]{0:T(256)S(1)} %get-tuple-element.20, s32[512]{0:T(512)S(1)} %fusion.32, s32[256]{0:T(256)S(1)} %add_reduce_fusion, ...), kind=kOutput, calls=%fused_computation.1 | convolution fusion | flops 270139392 | bytes 2104320 | tf_op jit(solution)/shard_map/dot_general | solution.py:67
  82.8 5.6 %all-to-all-start.2 = ((bf16[16,16,1024]{2,1,0:T(8,128)(2,1)}), bf16[16,16,1024]{2,1,0:T(8,128)(2,1)S(1)}, u32[]{:S(2)}, u32[]{:S(2)}) async-start(bf16[16,16,1024]{2,1,0:T(8,128)(2,1)} %bitcast.15), calls=%async_computation.2 | async-start | bytes 1048576 | tf_op jit(solution)/shard_map/all_to_all | solution.py:68
  88.4 0.6 dynamic_slice.3
  89.0 9.5 %all-to-all-done.2 = bf16[16,16,1024]{2,1,0:T(8,128)(2,1)S(1)} async-done(((bf16[16,16,1024]{2,1,0:T(8,128)(2,1)}), bf16[16,16,1024]{2,1,0:T(8,128)(2,1)S(1)}, u32[]{:S(2)}, u32[]{:S(2)}) %all-to-all-start.2) | async-done | bytes 524320 | tf_op jit(solution)/shard_map/all_to_all | solution.py:68
  98.5 0.7 reduce_sum.92
  (27 shorter events, 0.4 us)
Async XLA Ops:
  2.2 15.3 %copy-start.1 = (s32[16]{0:T(128)S(1)}, s32[16]{0:T(128)}, u32[]{:S(2)}) copy-start(s32[16]{0:T(128)} %param.3) | copy-start | bytes 196
  2.2 15.5 %copy-start = (bf16[16,1024]{1,0:T(8,128)(2,1)S(1)}, bf16[16,1024]{1,0:T(8,128)(2,1)}, u32[]{:S(2)}) copy-start(bf16[16,1024]{1,0:T(8,128)(2,1)} %param.2) | copy-start | bytes 98308
  2.2 43.6 %all-to-all-start = ((bf16[16,16,1024]{2,1,0:T(8,128)(2,1)}), bf16[16,16,1024]{2,1,0:T(8,128)(2,1)S(1)}, u32[]{:S(2)}, u32[]{:S(2)}) async-start(bf16[16,16,1024]{2,1,0:T(8,128)(2,1)} %broadcast_in_dim.17), calls=%async_computation | async-start | bytes 1048576 | tf_op jit(solution)/shard_map/all_to_all | solution.py:24
  45.8 3.8 %collective-permute-start = (bf16[256,1024]{1,0:T(8,128)(2,1)S(1)}, bf16[256,1024]{1,0:T(8,128)(2,1)S(1)}, u32[]{:S(2)}, u32[]{:S(2)}) collective-permute-start(bf16[256,1024]{1,0:T(8,128)(2,1)S(1)} %bitcast.39), channel_id=1, source_target_pairs={{0,1},{1,0},{2,3},{3,2},{4,5},{5,4},{6,7},{7,6},{8,9},{9,8},{10,11... | collective-permute-start | bytes 1572872 | tf_op jit(solution)/shard_map/ppermute | solution.py:29
  51.3 29.9 %all-to-all-start.1 = ((f32[32,4,128]{2,1,0:T(4,128)}), f32[32,4,128]{2,1,0:T(4,128)S(1)}, u32[]{:S(2)}, u32[]{:S(2)}) async-start(f32[32,4,128]{2,1,0:T(4,128)} %broadcast_in_dim.19), calls=%async_computation.1 | async-start | bytes 131072 | tf_op jit(solution)/shard_map/all_to_all | solution.py:53
  82.8 15.7 %all-to-all-start.2 = ((bf16[16,16,1024]{2,1,0:T(8,128)(2,1)}), bf16[16,16,1024]{2,1,0:T(8,128)(2,1)S(1)}, u32[]{:S(2)}, u32[]{:S(2)}) async-start(bf16[16,16,1024]{2,1,0:T(8,128)(2,1)} %bitcast.15), calls=%async_computation.2 | async-start | bytes 1048576 | tf_op jit(solution)/shard_map/all_to_all | solution.py:68

commit v5 on v4

--- a/solution.py
+++ b/solution.py
@@ -14,6 +14,12 @@
 
 def combine(stats):
     return jnp.stack([jax.nn.logsumexp(stats[:, 0], axis=0), jnp.sum(stats[:, 1], axis=0)])
+
+
+def slots(stats, axis):
+    n = lax.axis_size(axis)
+    mine = jnp.arange(n)[:, None, None] == lax.axis_index(axis)
+    return lax.psum(jnp.where(mine, stats[None], 0.0), axis)
 
 
 def local(views, partner):
@@ -51,8 +57,8 @@
     column_out = jnp.broadcast_to(swap(column_part).reshape(1, 4, 128), (32, 4, 128))
     row_stats = jnp.stack([row_part, picked])
     column_stats = lax.all_to_all(column_out, LINE + ("core",), 0, 0)
-    row_stats = combine(lax.all_gather(row_stats, "x"))
-    row_stats = lax.all_gather(row_stats, "y")
+    row_stats = combine(slots(row_stats, "x"))
+    row_stats = slots(row_stats, "y")
     row_stats, column_stats = lax.optimization_barrier((row_stats, column_stats))
     row_lse, picked = combine(row_stats)
     column_lse = swap(jax.nn.logsumexp(column_stats.reshape(32, 512), axis=0))

time: 99.8 us -> 96.8 us (0.970)
  blocking collectives: 45.6 us -> 43.9 us
  starting transfers between devices: 31.8 us -> 30.4 us
    all_gather x2 -> x0, blocking collectives: 20.8 us -> none  [the longest x1 10.4 us: local(): row_stats = combine(lax.all_gather(row_stats, 'x'))]
    psum x0 -> x2, blocking collectives: none -> 19.1 us  [slots(): return lax.psum(jnp.where(mine, stats[None], 0.0), axis)]
    all_to_all x1, starting transfers between devices: 5.63 us -> 3.57 us  [local(): lax.all_to_all(term.astype(jnp.bfloat16).reshape(16, shard, width), PLANE...]
where the time goes in v5:
time: 96.8 us; the launch traced here: 96.2 us
  blocking collectives  43.9 us (45%)
  starting transfers between devices  30.4 us (31%)
  waiting for transfers between devices  13.8 us (14%)
  local copies, waits for them, and re-layouts  3.6 us (4%)
  matrix products  1.98 us (2%)
  other arithmetic  1.75 us (2%)
    all_gather x1, blocking collectives, local(): rows = lax.all_gather(packed, PLANE, axis=0, tiled=True)  24.8 us
    psum x2, blocking collectives, slots(): return lax.psum(jnp.where(mine, stats[None], 0.0), axis)  19.1 us
    all_to_all x1, starting transfers between devices, local(): lax.all_to_all(jnp.broadcast_to(views[None], (16, shard, width)), LINE, 0...  15.3 us
    all_to_all x1, starting transfers between devices, local(): column_stats = lax.all_to_all(column_out, LINE + ('core',), 0, 0)  9.56 us
    all_to_all x1, waiting for transfers between devices, local(): lax.all_to_all(term.astype(jnp.bfloat16).reshape(16, shard, width), PLANE...  9.47 us
    all_to_all x1, starting transfers between devices, local(): lax.all_to_all(term.astype(jnp.bfloat16).reshape(16, shard, width), PLANE...  3.57 us
    all_to_all x1, waiting for transfers between devices, local(): lax.all_to_all(jnp.broadcast_to(views[None], (16, shard, width)), LINE, 0...  2.68 us
  transfers between devices with their start and end apart: 4, of which 3 were waited for; matrix products, arithmetic and copies ran while one was open for 1% of the time, Pallas kernels for 0%

profile of v5, /device:TPU:32, one launch (start us, length us, event | category | flops | bytes accessed | tf_op | source)
XLA Modules:
  0.0 96.2 jit_solution(9547739302482594819)
XLA Ops:
  0.6 1.6 %broadcast_in_dim.72 = bf16[16,16,1024]{2,1,0:T(8,128)(2,1)} broadcast(bf16[16,1024]{1,0:T(8,128)(2,1)} %param.2), dimensions={1,2} | broadcast | bytes 557056 | tf_op jit(solution)/shard_map/broadcast_in_dim | solution.py:30
  2.2 0.0 copy-start.1
  2.2 15.3 %all-to-all-start = ((bf16[16,16,1024]{2,1,0:T(8,128)(2,1)}), bf16[16,16,1024]{2,1,0:T(8,128)(2,1)S(1)}, u32[]{:S(2)}, u32[]{:S(2)}) async-start(bf16[16,16,1024]{2,1,0:T(8,128)(2,1)} %broadcast_in_dim.72), calls=%async_computation | async-start | bytes 1048576 | tf_op jit(solution)/shard_map/all_to_all | solution.py:30
  17.6 0.0 copy-start
  17.6 0.0 copy-done.1
  17.6 0.1 copy.10
  17.7 0.6 copy-done
  18.3 24.8 %all_gather.3 = bf16[256,1152]{1,0:T(8,128)(2,1)S(1)} all-gather(bf16[16,1152]{1,0:T(8,128)(2,1)S(1)} %fusion.17), channel_id=1, replica_groups=mesh['zh'=2,'x'=4,'y'=4,'zl'=8,'core'=2] {'x','y'}, dimensions={0}, use_global_device_ids=true | all-gather | bytes 626688 | tf_op jit(solution)/shard_map/all_gather | solution.py:31
  43.1 2.7 %all-to-all-done = bf16[16,16,1024]{2,1,0:T(8,128)(2,1)S(1)} async-done(((bf16[16,16,1024]{2,1,0:T(8,128)(2,1)}), bf16[16,16,1024]{2,1,0:T(8,128)(2,1)S(1)}, u32[]{:S(2)}, u32[]{:S(2)}) %all-to-all-start) | async-done | bytes 524320 | tf_op jit(solution)/shard_map/all_to_all | solution.py:30
  45.8 1.9 %collective-permute-start = (bf16[256,1024]{1,0:T(8,128)(2,1)S(1)}, bf16[256,1024]{1,0:T(8,128)(2,1)S(1)}, u32[]{:S(2)}, u32[]{:S(2)}) collective-permute-start(bf16[256,1024]{1,0:T(8,128)(2,1)S(1)} %bitcast.35), channel_id=1, source_target_pairs={{0,1},{1,0},{2,3},{3,2},{4,5},{5,4},{6,7},{7,6},{8,9},{9,8},{10,11... | collective-permute-start | bytes 1572872 | tf_op jit(solution)/shard_map/ppermute | solution.py:35
  47.8 0.2 add_reduce_fusion
  48.0 1.6 %collective-permute-done = bf16[256,1024]{1,0:T(8,128)(2,1)S(1)} collective-permute-done((bf16[256,1024]{1,0:T(8,128)(2,1)S(1)}, bf16[256,1024]{1,0:T(8,128)(2,1)S(1)}, u32[]{:S(2)}, u32[]{:S(2)}) %collective-permute-start) | collective-permute-done | bytes 524320 | tf_op jit(solution)/shard_map/ppermute | solution.py:35
  49.6 0.6 fusion.5
  50.2 0.4 exponential_reduce_fusion
  50.6 0.6 broadcast_in_dim.77
  51.3 9.6 %all-to-all-start.1 = ((f32[32,4,128]{2,1,0:T(4,128)}), f32[32,4,128]{2,1,0:T(4,128)S(1)}, u32[]{:S(2)}, u32[]{:S(2)}) async-start(f32[32,4,128]{2,1,0:T(4,128)} %broadcast_in_dim.77), calls=%async_computation.1 | async-start | bytes 131072 | tf_op jit(solution)/shard_map/all_to_all | solution.py:59
  60.9 0.1 broadcast_select_fusion.1
  60.9 9.8 %psum.14 = f32[4,2,256]{2,0,1:T(4,128)S(1)} all-reduce(f32[4,2,256]{2,0,1:T(4,128)S(1)} %broadcast_select_fusion.1), channel_id=1, replica_groups=mesh['zh'=2,'x'=4,'y'=4,'zl'=8,'core'=2] {'x'}, use_global_device_ids=true, to_apply=%region_3.4 | all-reduce | flops 2048 | bytes 16384 | tf_op jit(solution)/shard_map/psum | solution.py:22
  70.8 0.1 broadcast_select_fusion
  70.9 9.4 %psum.15 = f32[4,2,256]{2,0,1:T(4,128)S(1)} all-reduce(f32[4,2,256]{2,0,1:T(4,128)S(1)} %broadcast_select_fusion), channel_id=1, replica_groups=mesh['zh'=2,'x'=4,'y'=4,'zl'=8,'core'=2] {'y'}, use_global_device_ids=true, to_apply=%region_7.8 | all-reduce | flops 2048 | bytes 16384 | tf_op jit(solution)/shard_map/psum | solution.py:22
  80.3 0.0 all-to-all-done.1
  80.3 0.1 exponential_reduce_fusion.2
  80.5 1.4 %fusion = bf16[256,1024]{1,0:T(8,128)(2,1)} fusion(bf16[512,1024]{1,0:T(8,128)(2,1)S(1)} %constant_dynamic-update-slice_fusion, f32[256,512]{1,0:T(8,128)S(1)} %get-tuple-element.27, f32[512]{0:T(512)S(1)} %maximum_select_fusion.1, f32[256]{0:T(256)S(1)} %get-tuple-element.20, s32[512]{0:T(512)S(1)} %fusion.32, s32[256]{0:T(256)S(1)} %add_reduce_fusion, ...), kind=kOutput, calls=%fused_computation.1 | convolution fusion | flops 270139392 | bytes 2104320 | tf_op jit(solution)/shard_map/dot_general | solution.py:73
  81.9 3.6 %all-to-all-start.2 = ((bf16[16,16,1024]{2,1,0:T(8,128)(2,1)}), bf16[16,16,1024]{2,1,0:T(8,128)(2,1)S(1)}, u32[]{:S(2)}, u32[]{:S(2)}) async-start(bf16[16,16,1024]{2,1,0:T(8,128)(2,1)} %bitcast.15), calls=%async_computation.2 | async-start | bytes 1048576 | tf_op jit(solution)/shard_map/all_to_all | solution.py:74
  85.5 0.6 dynamic_slice.3
  86.1 9.5 %all-to-all-done.2 = bf16[16,16,1024]{2,1,0:T(8,128)(2,1)S(1)} async-done(((bf16[16,16,1024]{2,1,0:T(8,128)(2,1)}), bf16[16,16,1024]{2,1,0:T(8,128)(2,1)S(1)}, u32[]{:S(2)}, u32[]{:S(2)}) %all-to-all-start.2) | async-done | bytes 524320 | tf_op jit(solution)/shard_map/all_to_all | solution.py:74
  95.5 0.7 reduce_sum.92
  (29 shorter events, 0.4 us)
Async XLA Ops:
  2.2 15.4 %copy-start.1 = (s32[16]{0:T(128)S(1)}, s32[16]{0:T(128)}, u32[]{:S(2)}) copy-start(s32[16]{0:T(128)} %param.3) | copy-start | bytes 196
  2.2 43.6 %all-to-all-start = ((bf16[16,16,1024]{2,1,0:T(8,128)(2,1)}), bf16[16,16,1024]{2,1,0:T(8,128)(2,1)S(1)}, u32[]{:S(2)}, u32[]{:S(2)}) async-start(bf16[16,16,1024]{2,1,0:T(8,128)(2,1)} %broadcast_in_dim.72), calls=%async_computation | async-start | bytes 1048576 | tf_op jit(solution)/shard_map/all_to_all | solution.py:30
  17.6 0.8 copy-start
  45.8 3.8 %collective-permute-start = (bf16[256,1024]{1,0:T(8,128)(2,1)S(1)}, bf16[256,1024]{1,0:T(8,128)(2,1)S(1)}, u32[]{:S(2)}, u32[]{:S(2)}) collective-permute-start(bf16[256,1024]{1,0:T(8,128)(2,1)S(1)} %bitcast.35), channel_id=1, source_target_pairs={{0,1},{1,0},{2,3},{3,2},{4,5},{5,4},{6,7},{7,6},{8,9},{9,8},{10,11... | collective-permute-start | bytes 1572872 | tf_op jit(solution)/shard_map/ppermute | solution.py:35
  51.3 29.0 %all-to-all-start.1 = ((f32[32,4,128]{2,1,0:T(4,128)}), f32[32,4,128]{2,1,0:T(4,128)S(1)}, u32[]{:S(2)}, u32[]{:S(2)}) async-start(f32[32,4,128]{2,1,0:T(4,128)} %broadcast_in_dim.77), calls=%async_computation.1 | async-start | bytes 131072 | tf_op jit(solution)/shard_map/all_to_all | solution.py:59
  81.9 13.6 %all-to-all-start.2 = ((bf16[16,16,1024]{2,1,0:T(8,128)(2,1)}), bf16[16,16,1024]{2,1,0:T(8,128)(2,1)S(1)}, u32[]{:S(2)}, u32[]{:S(2)}) async-start(bf16[16,16,1024]{2,1,0:T(8,128)(2,1)} %bitcast.15), calls=%async_computation.2 | async-start | bytes 1048576 | tf_op jit(solution)/shard_map/all_to_all | solution.py:74

commit v6 on v5

--- a/solution.py
+++ b/solution.py
@@ -10,6 +10,8 @@
 NAMES = ("zh", "x", "y", "zl", "core")
 PLANE = ("x", "y")
 LINE = ("zh", "zl")
+FIRST = 13
+ORDER = [[(FIRST + i) % 16 for i in range(16)]]
 
 
 def combine(stats):
@@ -27,7 +29,9 @@
     width = views.shape[1]
     digits = jnp.stack([partner // 128, partner % 128], axis=1).astype(jnp.bfloat16)
     packed = jnp.concatenate([views, jnp.pad(digits, ((0, 0), (0, 126)))], axis=1)
-    line = lax.all_to_all(jnp.broadcast_to(views[None], (16, shard, width)), LINE, 0, 0)
+    line = lax.all_to_all(
+        jnp.broadcast_to(views[None], (16, shard, width)), LINE, 0, 0, axis_index_groups=ORDER
+    )
     rows = lax.all_gather(packed, PLANE, axis=0, tiled=True)
     line, rows = lax.optimization_barrier((line.reshape(256, width), rows))
     row_views = rows[:, :width]
@@ -41,7 +45,8 @@
     r = jnp.arange(256, dtype=jnp.int32)
     row_ids = ((zh * 16 + r // 16) * 16 + zl * 2 + core) * 16 + r % 16
     c = jnp.arange(512, dtype=jnp.int32)
-    column_ids = ((c // 128 % 2 * 16 + x * 4 + y) * 16 + c // 16 % 8 * 2 + (core ^ (c // 256))) * 16 + c % 16
+    z = (c // 16 + FIRST) % 16
+    column_ids = ((z // 8 * 16 + x * 4 + y) * 16 + z % 8 * 2 + (core ^ (c // 256))) * 16 + c % 16
 
     scores = inverse_softness * jnp.dot(
         row_views, column_views.T, preferred_element_type=jnp.float32

time: 96.8 us -> 96.4 us (level)
  waiting for transfers between devices: 13.8 us -> 11.1 us
  blocking collectives: 43.9 us -> 46.2 us
    all_to_all x1, waiting for transfers between devices: 2.68 us -> 0.01 us  [local(): lax.all_to_all(jnp.broadcast_to(views[None], (16, shard, width)), LINE, 0...]
    psum x2, blocking collectives: 19.1 us -> 21.4 us  [slots(): return lax.psum(jnp.where(mine, stats[None], 0.0), axis)]
  transfers between devices with their start and end apart: 4 -> 4, of which waited for: 3 -> 2; matrix products, arithmetic and copies ran while one was open for 1% -> 1% of each run, Pallas kernels for 0% -> 0%
where the time goes in v6:
time: 96.4 us; the launch traced here: 95.8 us
  blocking collectives  46.2 us (48%)
  starting transfers between devices  30.3 us (31%)
  waiting for transfers between devices  11.1 us (12%)
  local copies, waits for them, and re-layouts  3.6 us (4%)
  matrix products  1.98 us (2%)
  other arithmetic  1.75 us (2%)
    all_gather x1, blocking collectives, local(): rows = lax.all_gather(packed, PLANE, axis=0, tiled=True)  24.8 us
    psum x2, blocking collectives, slots(): return lax.psum(jnp.where(mine, stats[None], 0.0), axis)  21.4 us
    all_to_all x1, starting transfers between devices, local(): lax.all_to_all(jnp.broadcast_to(views[None], (16, shard, width)), LINE, 0...  15.3 us
    all_to_all x1, starting transfers between devices, local(): column_stats = lax.all_to_all(column_out, LINE + ('core',), 0, 0)  9.49 us
    all_to_all x1, waiting for transfers between devices, local(): lax.all_to_all(term.astype(jnp.bfloat16).reshape(16, shard, width), PLANE...  9.47 us
    all_to_all x1, starting transfers between devices, local(): lax.all_to_all(term.astype(jnp.bfloat16).reshape(16, shard, width), PLANE...  3.57 us
  transfers between devices with their start and end apart: 4, of which 2 were waited for; matrix products, arithmetic and copies ran while one was open for 1% of the time, Pallas kernels for 0%

profile of v6, /device:TPU:32, one launch (start us, length us, event | category | flops | bytes accessed | tf_op | source)
XLA Modules:
  0.0 95.8 jit_solution(15504061554302152501)
XLA Ops:
  0.6 1.6 %broadcast_in_dim.72 = bf16[16,16,1024]{2,1,0:T(8,128)(2,1)} broadcast(bf16[16,1024]{1,0:T(8,128)(2,1)} %param.2), dimensions={1,2} | broadcast | bytes 557056 | tf_op jit(solution)/shard_map/broadcast_in_dim | solution.py:33
  2.2 0.0 copy-start.1
  2.2 15.3 %all-to-all-start = ((bf16[16,16,1024]{2,1,0:T(8,128)(2,1)}), bf16[16,16,1024]{2,1,0:T(8,128)(2,1)S(1)}, u32[]{:S(2)}, u32[]{:S(2)}) async-start(bf16[16,16,1024]{2,1,0:T(8,128)(2,1)} %broadcast_in_dim.72), calls=%async_computation | async-start | bytes 1048576 | tf_op jit(solution)/shard_map/all_to_all | solution.py:32
  17.6 0.0 copy-start
  17.6 0.0 copy-done.1
  17.6 0.1 copy.10
  17.7 0.6 copy-done
  18.3 24.8 %all_gather.3 = bf16[256,1152]{1,0:T(8,128)(2,1)S(1)} all-gather(bf16[16,1152]{1,0:T(8,128)(2,1)S(1)} %fusion.17), channel_id=1, replica_groups=mesh['zh'=2,'x'=4,'y'=4,'zl'=8,'core'=2] {'x','y'}, dimensions={0}, use_global_device_ids=true | all-gather | bytes 626688 | tf_op jit(solution)/shard_map/all_gather | solution.py:35
  43.2 0.0 all-to-all-done
  43.2 1.9 %collective-permute-start = (bf16[256,1024]{1,0:T(8,128)(2,1)S(1)}, bf16[256,1024]{1,0:T(8,128)(2,1)S(1)}, u32[]{:S(2)}, u32[]{:S(2)}) collective-permute-start(bf16[256,1024]{1,0:T(8,128)(2,1)S(1)} %bitcast.35), channel_id=1, source_target_pairs={{0,1},{1,0},{2,3},{3,2},{4,5},{5,4},{6,7},{7,6},{8,9},{9,8},{10,11... | collective-permute-start | bytes 1572872 | tf_op jit(solution)/shard_map/ppermute | solution.py:39
  45.1 0.2 add_reduce_fusion
  45.4 1.6 %collective-permute-done = bf16[256,1024]{1,0:T(8,128)(2,1)S(1)} collective-permute-done((bf16[256,1024]{1,0:T(8,128)(2,1)S(1)}, bf16[256,1024]{1,0:T(8,128)(2,1)S(1)}, u32[]{:S(2)}, u32[]{:S(2)}) %collective-permute-start) | collective-permute-done | bytes 524320 | tf_op jit(solution)/shard_map/ppermute | solution.py:39
  47.0 0.6 fusion.5
  47.6 0.4 exponential_reduce_fusion
  48.0 0.6 broadcast_in_dim.77
  48.6 9.5 %all-to-all-start.1 = ((f32[32,4,128]{2,1,0:T(4,128)}), f32[32,4,128]{2,1,0:T(4,128)S(1)}, u32[]{:S(2)}, u32[]{:S(2)}) async-start(f32[32,4,128]{2,1,0:T(4,128)} %broadcast_in_dim.77), calls=%async_computation.1 | async-start | bytes 131072 | tf_op jit(solution)/shard_map/all_to_all | solution.py:64
  58.2 0.1 broadcast_select_fusion.1
  58.2 10.6 %psum.14 = f32[4,2,256]{2,0,1:T(4,128)S(1)} all-reduce(f32[4,2,256]{2,0,1:T(4,128)S(1)} %broadcast_select_fusion.1), channel_id=1, replica_groups=mesh['zh'=2,'x'=4,'y'=4,'zl'=8,'core'=2] {'x'}, use_global_device_ids=true, to_apply=%region_3.4 | all-reduce | flops 2048 | bytes 16384 | tf_op jit(solution)/shard_map/psum | solution.py:24
  68.9 0.1 broadcast_select_fusion
  69.0 10.8 %psum.15 = f32[4,2,256]{2,0,1:T(4,128)S(1)} all-reduce(f32[4,2,256]{2,0,1:T(4,128)S(1)} %broadcast_select_fusion), channel_id=1, replica_groups=mesh['zh'=2,'x'=4,'y'=4,'zl'=8,'core'=2] {'y'}, use_global_device_ids=true, to_apply=%region_7.8 | all-reduce | flops 2048 | bytes 16384 | tf_op jit(solution)/shard_map/psum | solution.py:24
  79.8 0.0 all-to-all-done.1
  79.9 0.1 exponential_reduce_fusion.2
  80.0 1.4 %fusion = bf16[256,1024]{1,0:T(8,128)(2,1)} fusion(bf16[512,1024]{1,0:T(8,128)(2,1)S(1)} %constant_dynamic-update-slice_fusion, f32[256,512]{1,0:T(8,128)S(1)} %get-tuple-element.27, f32[512]{0:T(512)S(1)} %maximum_select_fusion.1, f32[256]{0:T(256)S(1)} %get-tuple-element.20, s32[512]{0:T(512)S(1)} %fusion.37, s32[256]{0:T(256)S(1)} %add_reduce_fusion, ...), kind=kOutput, calls=%fused_computation.1 | convolution fusion | flops 270139392 | bytes 2104320 | tf_op jit(solution)/shard_map/dot_general | solution.py:78
  81.4 3.6 %all-to-all-start.2 = ((bf16[16,16,1024]{2,1,0:T(8,128)(2,1)}), bf16[16,16,1024]{2,1,0:T(8,128)(2,1)S(1)}, u32[]{:S(2)}, u32[]{:S(2)}) async-start(bf16[16,16,1024]{2,1,0:T(8,128)(2,1)} %bitcast.15), calls=%async_computation.2 | async-start | bytes 1048576 | tf_op jit(solution)/shard_map/all_to_all | solution.py:79
  85.0 0.6 dynamic_slice.3
  85.6 9.5 %all-to-all-done.2 = bf16[16,16,1024]{2,1,0:T(8,128)(2,1)S(1)} async-done(((bf16[16,16,1024]{2,1,0:T(8,128)(2,1)}), bf16[16,16,1024]{2,1,0:T(8,128)(2,1)S(1)}, u32[]{:S(2)}, u32[]{:S(2)}) %all-to-all-start.2) | async-done | bytes 524320 | tf_op jit(solution)/shard_map/all_to_all | solution.py:79
  95.1 0.7 reduce_sum.92
  (29 shorter events, 0.4 us)
Async XLA Ops:
  2.2 15.4 %copy-start.1 = (s32[16]{0:T(128)S(1)}, s32[16]{0:T(128)}, u32[]{:S(2)}) copy-start(s32[16]{0:T(128)} %param.3) | copy-start | bytes 196
  2.2 40.9 %all-to-all-start = ((bf16[16,16,1024]{2,1,0:T(8,128)(2,1)}), bf16[16,16,1024]{2,1,0:T(8,128)(2,1)S(1)}, u32[]{:S(2)}, u32[]{:S(2)}) async-start(bf16[16,16,1024]{2,1,0:T(8,128)(2,1)} %broadcast_in_dim.72), calls=%async_computation | async-start | bytes 1048576 | tf_op jit(solution)/shard_map/all_to_all | solution.py:32
  17.6 0.8 copy-start
  43.2 3.8 %collective-permute-start = (bf16[256,1024]{1,0:T(8,128)(2,1)S(1)}, bf16[256,1024]{1,0:T(8,128)(2,1)S(1)}, u32[]{:S(2)}, u32[]{:S(2)}) collective-permute-start(bf16[256,1024]{1,0:T(8,128)(2,1)S(1)} %bitcast.35), channel_id=1, source_target_pairs={{0,1},{1,0},{2,3},{3,2},{4,5},{5,4},{6,7},{7,6},{8,9},{9,8},{10,11... | collective-permute-start | bytes 1572872 | tf_op jit(solution)/shard_map/ppermute | solution.py:39
  48.6 31.2 %all-to-all-start.1 = ((f32[32,4,128]{2,1,0:T(4,128)}), f32[32,4,128]{2,1,0:T(4,128)S(1)}, u32[]{:S(2)}, u32[]{:S(2)}) async-start(f32[32,4,128]{2,1,0:T(4,128)} %broadcast_in_dim.77), calls=%async_computation.1 | async-start | bytes 131072 | tf_op jit(solution)/shard_map/all_to_all | solution.py:64
  81.4 13.6 %all-to-all-start.2 = ((bf16[16,16,1024]{2,1,0:T(8,128)(2,1)}), bf16[16,16,1024]{2,1,0:T(8,128)(2,1)S(1)}, u32[]{:S(2)}, u32[]{:S(2)}) async-start(bf16[16,16,1024]{2,1,0:T(8,128)(2,1)} %bitcast.15), calls=%async_computation.2 | async-start | bytes 1048576 | tf_op jit(solution)/shard_map/all_to_all | solution.py:79

commit v7 on v6

--- a/solution.py
+++ b/solution.py
@@ -14,13 +14,9 @@
 ORDER = [[(FIRST + i) % 16 for i in range(16)]]
 
 
-def combine(stats):
-    return jnp.stack([jax.nn.logsumexp(stats[:, 0], axis=0), jnp.sum(stats[:, 1], axis=0)])
-
-
 def slots(stats, axis):
     n = lax.axis_size(axis)
-    mine = jnp.arange(n)[:, None, None] == lax.axis_index(axis)
+    mine = jnp.arange(n)[:, None] == lax.axis_index(axis)
     return lax.psum(jnp.where(mine, stats[None], 0.0), axis)
 
 
@@ -53,22 +49,24 @@
     )
     positive = column_ids[None, :] == rows_partner[:, None]
     masked = jnp.where(row_ids[:, None] == column_ids[None, :], very_low, scores)
-    picked = jnp.sum(jnp.where(positive, scores, 0.0), axis=1)
+    picked = jnp.sum(jnp.where(positive, scores, 0.0), axis=0)
     row_top = jnp.max(masked, axis=1)
     row_part = row_top + jnp.log(jnp.sum(jnp.exp(masked - row_top[:, None]), axis=1))
     column_top = jnp.max(masked, axis=0)
     column_part = column_top + jnp.log(jnp.sum(jnp.exp(masked - column_top[None, :]), axis=0))
 
-    column_out = jnp.broadcast_to(swap(column_part).reshape(1, 4, 128), (32, 4, 128))
-    row_stats = jnp.stack([row_part, picked])
+    column_out = jnp.stack([swap(column_part), swap(picked)]).reshape(1, 8, 128)
+    column_out = jnp.broadcast_to(column_out, (32, 8, 128))
     column_stats = lax.all_to_all(column_out, LINE + ("core",), 0, 0)
-    row_stats = combine(slots(row_stats, "x"))
-    row_stats = slots(row_stats, "y")
+    row_part = jax.nn.logsumexp(slots(row_part, "x"), axis=0)
+    row_stats = slots(row_part, "y")
     row_stats, column_stats = lax.optimization_barrier((row_stats, column_stats))
-    row_lse, picked = combine(row_stats)
-    column_lse = swap(jax.nn.logsumexp(column_stats.reshape(32, 512), axis=0))
-    loss = row_lse - picked
-    view_loss = lax.dynamic_slice_in_dim(loss, (x * 4 + y) * shard, shard, 0)
+    row_lse = jax.nn.logsumexp(row_stats, axis=0)
+    column_stats = column_stats.reshape(32, 2, 512)
+    column_lse = swap(jax.nn.logsumexp(column_stats[:, 0], axis=0))
+    loss = column_lse - swap(jnp.sum(column_stats[:, 1], axis=0))
+    here = (zh * 8 + zl - FIRST) % 16
+    view_loss = lax.dynamic_slice_in_dim(loss, here * shard, shard, 0)
 
     weight = (
         jnp.exp(masked - row_lse[:, None])

time: 96.4 us -> 96.3 us (level)
  no operation moved by 1% of the time
where the time goes in v7:
time: 96.3 us; the launch traced here: 95.7 us
  blocking collectives  46 us (48%)
  starting transfers between devices  30.3 us (31%)
  waiting for transfers between devices  11 us (11%)
  local copies, waits for them, and re-layouts  3.71 us (4%)
  matrix products  1.98 us (2%)
  other arithmetic  1.81 us (2%)
    all_gather x1, blocking collectives, local(): rows = lax.all_gather(packed, PLANE, axis=0, tiled=True)  24.8 us
    psum x2, blocking collectives, slots(): return lax.psum(jnp.where(mine, stats[None], 0.0), axis)  21.2 us
    all_to_all x1, starting transfers between devices, local(): lax.all_to_all(jnp.broadcast_to(views[None], (16, shard, width)), LINE, 0...  15.3 us
    all_to_all x1, starting transfers between devices, local(): column_stats = lax.all_to_all(column_out, LINE + ('core',), 0, 0)  9.49 us
    all_to_all x1, waiting for transfers between devices, local(): lax.all_to_all(term.astype(jnp.bfloat16).reshape(16, shard, width), PLANE...  9.44 us
    all_to_all x1, starting transfers between devices, local(): lax.all_to_all(term.astype(jnp.bfloat16).reshape(16, shard, width), PLANE...  3.57 us
  transfers between devices with their start and end apart: 4, of which 2 were waited for; matrix products, arithmetic and copies ran while one was open for 1% of the time, Pallas kernels for 0%

profile of v7, /device:TPU:32, one launch (start us, length us, event | category | flops | bytes accessed | tf_op | source)
XLA Modules:
  0.0 95.7 jit_solution(14119729713309234775)
XLA Ops:
  0.6 1.6 %broadcast_in_dim.73 = bf16[16,16,1024]{2,1,0:T(8,128)(2,1)} broadcast(bf16[16,1024]{1,0:T(8,128)(2,1)} %param.2), dimensions={1,2} | broadcast | bytes 557056 | tf_op jit(solution)/shard_map/broadcast_in_dim | solution.py:29
  2.2 0.0 copy-start.1
  2.2 15.3 %all-to-all-start = ((bf16[16,16,1024]{2,1,0:T(8,128)(2,1)}), bf16[16,16,1024]{2,1,0:T(8,128)(2,1)S(1)}, u32[]{:S(2)}, u32[]{:S(2)}) async-start(bf16[16,16,1024]{2,1,0:T(8,128)(2,1)} %broadcast_in_dim.73), calls=%async_computation | async-start | bytes 1048576 | tf_op jit(solution)/shard_map/all_to_all | solution.py:28
  17.6 0.0 copy-start
  17.6 0.0 copy-done.1
  17.6 0.1 copy.13
  17.7 0.6 copy-done
  18.3 24.8 %all_gather.3 = bf16[256,1152]{1,0:T(8,128)(2,1)S(1)} all-gather(bf16[16,1152]{1,0:T(8,128)(2,1)S(1)} %fusion.19), channel_id=1, replica_groups=mesh['zh'=2,'x'=4,'y'=4,'zl'=8,'core'=2] {'x','y'}, dimensions={0}, use_global_device_ids=true | all-gather | bytes 626688 | tf_op jit(solution)/shard_map/all_gather | solution.py:31
  43.2 0.0 all-to-all-done
  43.2 1.9 %collective-permute-start = (bf16[256,1024]{1,0:T(8,128)(2,1)S(1)}, bf16[256,1024]{1,0:T(8,128)(2,1)S(1)}, u32[]{:S(2)}, u32[]{:S(2)}) collective-permute-start(bf16[256,1024]{1,0:T(8,128)(2,1)S(1)} %bitcast.20), channel_id=1, source_target_pairs={{0,1},{1,0},{2,3},{3,2},{4,5},{5,4},{6,7},{7,6},{8,9},{9,8},{10,11... | collective-permute-start | bytes 1572872 | tf_op jit(solution)/shard_map/ppermute | solution.py:35
  45.1 0.2 add_reduce_fusion
  45.4 1.6 %collective-permute-done = bf16[256,1024]{1,0:T(8,128)(2,1)S(1)} collective-permute-done((bf16[256,1024]{1,0:T(8,128)(2,1)S(1)}, bf16[256,1024]{1,0:T(8,128)(2,1)S(1)}, u32[]{:S(2)}, u32[]{:S(2)}) %collective-permute-start) | collective-permute-done | bytes 524320 | tf_op jit(solution)/shard_map/ppermute | solution.py:35
  47.0 0.6 fusion.5
  47.6 0.4 exponential_reduce_fusion
  48.0 0.6 broadcast_in_dim.79
  48.7 9.5 %all-to-all-start.1 = ((f32[32,8,128]{2,1,0:T(8,128)}), f32[32,8,128]{2,1,0:T(8,128)S(1)}, u32[]{:S(2)}, u32[]{:S(2)}) async-start(f32[32,8,128]{2,1,0:T(8,128)} %broadcast_in_dim.79), calls=%async_computation.1 | async-start | bytes 262144 | tf_op jit(solution)/shard_map/all_to_all | solution.py:60
  58.2 0.1 broadcast_select_fusion.3
  58.2 10.5 %psum.14 = f32[4,256]{1,0:T(4,128)S(1)} all-reduce(f32[4,256]{1,0:T(4,128)S(1)} %broadcast_select_fusion.3), channel_id=1, replica_groups=mesh['zh'=2,'x'=4,'y'=4,'zl'=8,'core'=2] {'x'}, use_global_device_ids=true, to_apply=%region_2.3 | all-reduce | flops 1024 | bytes 8192 | tf_op jit(solution)/shard_map/psum | solution.py:20
  68.8 0.1 broadcast_select_fusion.2
  68.9 10.7 %psum.15 = f32[4,256]{1,0:T(4,128)S(1)} all-reduce(f32[4,256]{1,0:T(4,128)S(1)} %broadcast_select_fusion.2), channel_id=1, replica_groups=mesh['zh'=2,'x'=4,'y'=4,'zl'=8,'core'=2] {'y'}, use_global_device_ids=true, to_apply=%region_5.6 | all-reduce | flops 1024 | bytes 8192 | tf_op jit(solution)/shard_map/psum | solution.py:20
  79.6 0.0 all-to-all-done.1
  79.6 0.1 reshape.265
  79.7 0.1 slice_reduce_fusion
  80.0 1.4 %fusion = bf16[256,1024]{1,0:T(8,128)(2,1)} fusion(bf16[512,1024]{1,0:T(8,128)(2,1)S(1)} %constant_dynamic-update-slice_fusion, f32[256,512]{1,0:T(8,128)S(1)} %get-tuple-element.30, f32[512]{0:T(512)S(1)} %get-tuple-element.18, f32[256]{0:T(256)S(1)} %log_add_fusion.2, s32[512]{0:T(512)S(1)} %fusion.35, s32[256]{0:T(256)S(1)} %add_reduce_fusion, ...), kind=kOutput, calls=%fused_computation.1 | convolution fusion | flops 270139392 | bytes 2104320 | tf_op jit(solution)/shard_map/dot_general | solution.py:76
  81.4 3.6 %all-to-all-start.2 = ((bf16[16,16,1024]{2,1,0:T(8,128)(2,1)}), bf16[16,16,1024]{2,1,0:T(8,128)(2,1)S(1)}, u32[]{:S(2)}, u32[]{:S(2)}) async-start(bf16[16,16,1024]{2,1,0:T(8,128)(2,1)} %bitcast.9), calls=%async_computation.2 | async-start | bytes 1048576 | tf_op jit(solution)/shard_map/all_to_all | solution.py:77
  85.0 0.6 dynamic_slice.3
  85.6 9.4 %all-to-all-done.2 = bf16[16,16,1024]{2,1,0:T(8,128)(2,1)S(1)} async-done(((bf16[16,16,1024]{2,1,0:T(8,128)(2,1)}), bf16[16,16,1024]{2,1,0:T(8,128)(2,1)S(1)}, u32[]{:S(2)}, u32[]{:S(2)}) %all-to-all-start.2) | async-done | bytes 524320 | tf_op jit(solution)/shard_map/all_to_all | solution.py:77
  95.0 0.7 reduce_sum.85
  (30 shorter events, 0.4 us)
Async XLA Ops:
  2.2 15.4 %copy-start.1 = (s32[16]{0:T(128)S(1)}, s32[16]{0:T(128)}, u32[]{:S(2)}) copy-start(s32[16]{0:T(128)} %param.3) | copy-start | bytes 196
  2.2 40.9 %all-to-all-start = ((bf16[16,16,1024]{2,1,0:T(8,128)(2,1)}), bf16[16,16,1024]{2,1,0:T(8,128)(2,1)S(1)}, u32[]{:S(2)}, u32[]{:S(2)}) async-start(bf16[16,16,1024]{2,1,0:T(8,128)(2,1)} %broadcast_in_dim.73), calls=%async_computation | async-start | bytes 1048576 | tf_op jit(solution)/shard_map/all_to_all | solution.py:28
  17.6 0.8 copy-start
  43.2 3.8 %collective-permute-start = (bf16[256,1024]{1,0:T(8,128)(2,1)S(1)}, bf16[256,1024]{1,0:T(8,128)(2,1)S(1)}, u32[]{:S(2)}, u32[]{:S(2)}) collective-permute-start(bf16[256,1024]{1,0:T(8,128)(2,1)S(1)} %bitcast.20), channel_id=1, source_target_pairs={{0,1},{1,0},{2,3},{3,2},{4,5},{5,4},{6,7},{7,6},{8,9},{9,8},{10,11... | collective-permute-start | bytes 1572872 | tf_op jit(solution)/shard_map/ppermute | solution.py:35
  48.7 30.9 %all-to-all-start.1 = ((f32[32,8,128]{2,1,0:T(8,128)}), f32[32,8,128]{2,1,0:T(8,128)S(1)}, u32[]{:S(2)}, u32[]{:S(2)}) async-start(f32[32,8,128]{2,1,0:T(8,128)} %broadcast_in_dim.79), calls=%async_computation.1 | async-start | bytes 262144 | tf_op jit(solution)/shard_map/all_to_all | solution.py:60
  81.4 13.6 %all-to-all-start.2 = ((bf16[16,16,1024]{2,1,0:T(8,128)(2,1)}), bf16[16,16,1024]{2,1,0:T(8,128)(2,1)S(1)}, u32[]{:S(2)}, u32[]{:S(2)}) async-start(bf16[16,16,1024]{2,1,0:T(8,128)(2,1)} %bitcast.9), calls=%async_computation.2 | async-start | bytes 1048576 | tf_op jit(solution)/shard_map/all_to_all | solution.py:77

commit v8 on v7

--- a/solution.py
+++ b/solution.py
@@ -11,6 +11,7 @@
 PLANE = ("x", "y")
 LINE = ("zh", "zl")
 FIRST = 13
+PAIRS = [[(4 + i) % 32 for i in range(32)]]
 ORDER = [[(FIRST + i) % 16 for i in range(16)]]
 
 
@@ -57,7 +58,9 @@
 
     column_out = jnp.stack([swap(column_part), swap(picked)]).reshape(1, 8, 128)
     column_out = jnp.broadcast_to(column_out, (32, 8, 128))
-    column_stats = lax.all_to_all(column_out, LINE + ("core",), 0, 0)
+    column_stats = lax.all_to_all(
+        column_out, LINE + ("core",), 0, 0, axis_index_groups=PAIRS
+    )
     row_part = jax.nn.logsumexp(slots(row_part, "x"), axis=0)
     row_stats = slots(row_part, "y")
     row_stats, column_stats = lax.optimization_barrier((row_stats, column_stats))

time: 96.3 us -> 97.6 us (1.013)
  the two profiles are of different devices: /device:TPU:32 before, /device:TPU:8 now
where the time goes in v8:
time: 97.6 us; the launch traced here: 97 us
  blocking collectives  43.2 us (44%)
  starting transfers between devices  33.1 us (34%)
  waiting for transfers between devices  12.4 us (13%)
  local copies, waits for them, and re-layouts  3.7 us (4%)
  matrix products  1.98 us (2%)
  other arithmetic  1.81 us (2%)
    all_gather x1, blocking collectives, local(): rows = lax.all_gather(packed, PLANE, axis=0, tiled=True)  24 us
    psum x2, blocking collectives, slots(): return lax.psum(jnp.where(mine, stats[None], 0.0), axis)  19.1 us
    all_to_all x1, starting transfers between devices, local(): lax.all_to_all(jnp.broadcast_to(views[None], (16, shard, width)), LINE, 0...  15.8 us
    all_to_all x1, starting transfers between devices, local(): lax.all_to_all(column_out, LINE + ('core',), 0, 0, axis_index_groups=PAIRS)  9.56 us
    all_to_all x1, waiting for transfers between devices, local(): lax.all_to_all(term.astype(jnp.bfloat16).reshape(16, shard, width), PLANE...  8.24 us
    all_to_all x1, starting transfers between devices, local(): lax.all_to_all(term.astype(jnp.bfloat16).reshape(16, shard, width), PLANE...  5.85 us
    all_to_all x1, waiting for transfers between devices, local(): lax.all_to_all(jnp.broadcast_to(views[None], (16, shard, width)), LINE, 0...  2.59 us
  transfers between devices with their start and end apart: 4, of which 3 were waited for; matrix products, arithmetic and copies ran while one was open for 1% of the time, Pallas kernels for 0%

profile of v8, /device:TPU:8, one launch (start us, length us, event | category | flops | bytes accessed | tf_op | source)
XLA Modules:
  0.0 97.0 jit_solution(13404692396777899873)
XLA Ops:
  0.6 1.6 %broadcast_in_dim.73 = bf16[16,16,1024]{2,1,0:T(8,128)(2,1)} broadcast(bf16[16,1024]{1,0:T(8,128)(2,1)} %param.2), dimensions={1,2} | broadcast | bytes 557056 | tf_op jit(solution)/shard_map/broadcast_in_dim | solution.py:30
  2.2 0.0 copy-start.1
  2.2 15.8 %all-to-all-start = ((bf16[16,16,1024]{2,1,0:T(8,128)(2,1)}), bf16[16,16,1024]{2,1,0:T(8,128)(2,1)S(1)}, u32[]{:S(2)}, u32[]{:S(2)}) async-start(bf16[16,16,1024]{2,1,0:T(8,128)(2,1)} %broadcast_in_dim.73), calls=%async_computation | async-start | bytes 1048576 | tf_op jit(solution)/shard_map/all_to_all | solution.py:29
  18.0 0.0 copy-start
  18.1 0.0 copy-done.1
  18.1 0.1 copy.13
  18.2 0.6 copy-done
  18.8 24.0 %all_gather.3 = bf16[256,1152]{1,0:T(8,128)(2,1)S(1)} all-gather(bf16[16,1152]{1,0:T(8,128)(2,1)S(1)} %fusion.19), channel_id=1, replica_groups=mesh['zh'=2,'x'=4,'y'=4,'zl'=8,'core'=2] {'x','y'}, dimensions={0}, use_global_device_ids=true | all-gather | bytes 626688 | tf_op jit(solution)/shard_map/all_gather | solution.py:32
  42.8 2.6 %all-to-all-done = bf16[16,16,1024]{2,1,0:T(8,128)(2,1)S(1)} async-done(((bf16[16,16,1024]{2,1,0:T(8,128)(2,1)}), bf16[16,16,1024]{2,1,0:T(8,128)(2,1)S(1)}, u32[]{:S(2)}, u32[]{:S(2)}) %all-to-all-start) | async-done | bytes 524320 | tf_op jit(solution)/shard_map/all_to_all | solution.py:29
  45.4 1.9 %collective-permute-start = (bf16[256,1024]{1,0:T(8,128)(2,1)S(1)}, bf16[256,1024]{1,0:T(8,128)(2,1)S(1)}, u32[]{:S(2)}, u32[]{:S(2)}) collective-permute-start(bf16[256,1024]{1,0:T(8,128)(2,1)S(1)} %bitcast.20), channel_id=1, source_target_pairs={{0,1},{1,0},{2,3},{3,2},{4,5},{5,4},{6,7},{7,6},{8,9},{9,8},{10,11... | collective-permute-start | bytes 1572872 | tf_op jit(solution)/shard_map/ppermute | solution.py:36
  47.4 0.2 add_reduce_fusion
  47.6 1.6 %collective-permute-done = bf16[256,1024]{1,0:T(8,128)(2,1)S(1)} collective-permute-done((bf16[256,1024]{1,0:T(8,128)(2,1)S(1)}, bf16[256,1024]{1,0:T(8,128)(2,1)S(1)}, u32[]{:S(2)}, u32[]{:S(2)}) %collective-permute-start) | collective-permute-done | bytes 524320 | tf_op jit(solution)/shard_map/ppermute | solution.py:36
  49.3 0.6 fusion.5
  49.8 0.4 exponential_reduce_fusion
  50.3 0.6 broadcast_in_dim.79
  50.9 9.6 %all-to-all-start.1 = ((f32[32,8,128]{2,1,0:T(8,128)}), f32[32,8,128]{2,1,0:T(8,128)S(1)}, u32[]{:S(2)}, u32[]{:S(2)}) async-start(f32[32,8,128]{2,1,0:T(8,128)} %broadcast_in_dim.79), calls=%async_computation.1 | async-start | bytes 262144 | tf_op jit(solution)/shard_map/all_to_all | solution.py:61
  60.5 0.1 broadcast_select_fusion.3
  60.6 10.5 %psum.14 = f32[4,256]{1,0:T(4,128)S(1)} all-reduce(f32[4,256]{1,0:T(4,128)S(1)} %broadcast_select_fusion.3), channel_id=1, replica_groups=mesh['zh'=2,'x'=4,'y'=4,'zl'=8,'core'=2] {'x'}, use_global_device_ids=true, to_apply=%region_2.3 | all-reduce | flops 1024 | bytes 8192 | tf_op jit(solution)/shard_map/psum | solution.py:21
  71.1 0.1 broadcast_select_fusion.2
  71.2 8.7 %psum.15 = f32[4,256]{1,0:T(4,128)S(1)} all-reduce(f32[4,256]{1,0:T(4,128)S(1)} %broadcast_select_fusion.2), channel_id=1, replica_groups=mesh['zh'=2,'x'=4,'y'=4,'zl'=8,'core'=2] {'y'}, use_global_device_ids=true, to_apply=%region_5.6 | all-reduce | flops 1024 | bytes 8192 | tf_op jit(solution)/shard_map/psum | solution.py:21
  79.9 0.0 all-to-all-done.1
  79.9 0.1 reshape.265
  80.0 0.1 slice_reduce_fusion
  80.3 1.4 %fusion = bf16[256,1024]{1,0:T(8,128)(2,1)} fusion(bf16[512,1024]{1,0:T(8,128)(2,1)S(1)} %constant_dynamic-update-slice_fusion, f32[256,512]{1,0:T(8,128)S(1)} %get-tuple-element.30, f32[512]{0:T(512)S(1)} %get-tuple-element.18, f32[256]{0:T(256)S(1)} %log_add_fusion.2, s32[512]{0:T(512)S(1)} %fusion.35, s32[256]{0:T(256)S(1)} %add_reduce_fusion, ...), kind=kOutput, calls=%fused_computation.1 | convolution fusion | flops 270139392 | bytes 2104320 | tf_op jit(solution)/shard_map/dot_general | solution.py:79
  81.7 5.9 %all-to-all-start.2 = ((bf16[16,16,1024]{2,1,0:T(8,128)(2,1)}), bf16[16,16,1024]{2,1,0:T(8,128)(2,1)S(1)}, u32[]{:S(2)}, u32[]{:S(2)}) async-start(bf16[16,16,1024]{2,1,0:T(8,128)(2,1)} %bitcast.9), calls=%async_computation.2 | async-start | bytes 1048576 | tf_op jit(solution)/shard_map/all_to_all | solution.py:80
  87.5 0.6 dynamic_slice.3
  88.1 8.2 %all-to-all-done.2 = bf16[16,16,1024]{2,1,0:T(8,128)(2,1)S(1)} async-done(((bf16[16,16,1024]{2,1,0:T(8,128)(2,1)}), bf16[16,16,1024]{2,1,0:T(8,128)(2,1)S(1)}, u32[]{:S(2)}, u32[]{:S(2)}) %all-to-all-start.2) | async-done | bytes 524320 | tf_op jit(solution)/shard_map/all_to_all | solution.py:80
  96.3 0.7 reduce_sum.85
  (30 shorter events, 0.4 us)
Async XLA Ops:
  2.2 15.8 %copy-start.1 = (s32[16]{0:T(128)S(1)}, s32[16]{0:T(128)}, u32[]{:S(2)}) copy-start(s32[16]{0:T(128)} %param.3) | copy-start | bytes 196
  2.2 43.2 %all-to-all-start = ((bf16[16,16,1024]{2,1,0:T(8,128)(2,1)}), bf16[16,16,1024]{2,1,0:T(8,128)(2,1)S(1)}, u32[]{:S(2)}, u32[]{:S(2)}) async-start(bf16[16,16,1024]{2,1,0:T(8,128)(2,1)} %broadcast_in_dim.73), calls=%async_computation | async-start | bytes 1048576 | tf_op jit(solution)/shard_map/all_to_all | solution.py:29
  18.0 0.8 copy-start
  45.4 3.8 %collective-permute-start = (bf16[256,1024]{1,0:T(8,128)(2,1)S(1)}, bf16[256,1024]{1,0:T(8,128)(2,1)S(1)}, u32[]{:S(2)}, u32[]{:S(2)}) collective-permute-start(bf16[256,1024]{1,0:T(8,128)(2,1)S(1)} %bitcast.20), channel_id=1, source_target_pairs={{0,1},{1,0},{2,3},{3,2},{4,5},{5,4},{6,7},{7,6},{8,9},{9,8},{10,11... | collective-permute-start | bytes 1572872 | tf_op jit(solution)/shard_map/ppermute | solution.py:36
  50.9 28.9 %all-to-all-start.1 = ((f32[32,8,128]{2,1,0:T(8,128)}), f32[32,8,128]{2,1,0:T(8,128)S(1)}, u32[]{:S(2)}, u32[]{:S(2)}) async-start(f32[32,8,128]{2,1,0:T(8,128)} %broadcast_in_dim.79), calls=%async_computation.1 | async-start | bytes 262144 | tf_op jit(solution)/shard_map/all_to_all | solution.py:61
  81.7 14.7 %all-to-all-start.2 = ((bf16[16,16,1024]{2,1,0:T(8,128)(2,1)}), bf16[16,16,1024]{2,1,0:T(8,128)(2,1)S(1)}, u32[]{:S(2)}, u32[]{:S(2)}) async-start(bf16[16,16,1024]{2,1,0:T(8,128)(2,1)} %bitcast.9), calls=%async_computation.2 | async-start | bytes 1048576 | tf_op jit(solution)/shard_map/all_to_all | solution.py:80
